TPU v7x, 128 devices: a whole 4x4x4 slice. The times are simulated.
128 devices in a mesh: owner: 32 (over z, y, core), rep: 4 (over x).
Axes of the slice: x: 4, y: 4, z: 4, core: 2. Of those that a mesh axis runs over, the one named last changes fastest.
Arguments:
- paper_feat: bfloat16 [65536, 768], P('owner', 'rep'), may hold values from -6 to 6
- author_feat: bfloat16 [65536, 768], P('owner', 'rep'), may hold values from -6 to 6
- weights: bfloat16 [2, 768, 768], replicated, may hold values from -0.21875 to 0.21875
- relation: float32 [768], replicated, may hold values from -0.21875 to 0.21875
- send_rows: int32 [32, 32, 512], P('owner'), may hold values from 0 to 2047
- tile_src: int32 [1, 48, 512], P(None, None, 'owner'), may hold values from 0 to 127
- tile_col: int32 [1, 48, 65536], P(None, None, 'owner'), may hold values from 0 to 128, as said below
- cand_author: int32 [32768], P('owner'), may hold values from 0 to 2047
- cand_send: int32 [32, 32, 32], P('owner'), may hold values from 0 to 2047
- neg_rows: int32 [32, 32], P('owner'), may hold values from 0 to 2047
Outputs:
- refreshed: bfloat16 [65536, 768], P('owner', 'rep')
- edge_loss: float32 [32768], P('owner')
Inputs may be any that keep to these rules, and one draw needn't show every extreme that they name: `tile_col`: entry 128 marks an empty slot; an author's live slots in a relation are its first ones, from none to 48 of them.
All inputs are finite; a program needn't handle non-finite values.
Results may differ from a plain program's by a relative error of at most 0.0065.
Values may be sent and summed in bfloat16 or wider, within the bound.
A program may use at most 64 MiB of HBM per device.

v0:
```python
import jax
import jax.numpy as jnp
from jax import lax
from jax.sharding import PartitionSpec as P


def block_means(blocks, block_src, columns):
    block_count = blocks.shape[0]
    selector = (block_src[..., None] == jnp.arange(block_count, dtype=jnp.int32)).astype(
        jnp.bfloat16
    )
    picked = jnp.einsum(
        "rtb,bjc->rtjc", selector, blocks, preferred_element_type=jnp.float32
    ).astype(jnp.bfloat16)
    one_hot = (columns[..., None] == jnp.arange(128, dtype=jnp.int32)).astype(jnp.bfloat16)
    summed = jnp.einsum("rtij,rtjc->ric", one_hot, picked, preferred_element_type=jnp.float32)
    counted = jnp.sum((columns < 128).astype(jnp.float32), axis=1)
    return (summed / jnp.maximum(counted, 1.0)[..., None]).astype(jnp.bfloat16)


def per_device(
    paper_feat,
    author_feat,
    weights,
    relation,
    send_rows,
    tile_src,
    tile_col,
    cand_author,
    cand_send,
    neg_rows,
):
    width = paper_feat.shape[1]
    relations = tile_src.shape[0]
    author_rows = author_feat.shape[0]
    column_start = lax.axis_index("rep") * width
    outgoing = jnp.take(paper_feat, send_rows[0], axis=0)
    cand_out = jnp.take(paper_feat, cand_send[0], axis=0)
    received, cand_rows = (
        lax.all_to_all(outgoing, "owner", split_axis=0, concat_axis=0, tiled=True),
        lax.all_to_all(cand_out, "owner", split_axis=0, concat_axis=0, tiled=True),
    )
    blocks = received.reshape(-1, 128, width)
    cand_rows = cand_rows.reshape(-1, width)

    def one_block(block_id):
        block_src = lax.dynamic_index_in_dim(tile_src, block_id, 2, keepdims=False)
        columns = lax.dynamic_slice_in_dim(tile_col, block_id * 128, 128, 2)
        return block_means(blocks, block_src, columns)

    averages = lax.map(one_block, jnp.arange(tile_src.shape[2], dtype=jnp.int32))
    averages = averages.transpose(1, 0, 2, 3).reshape(relations, author_rows, width)
    local_weights = lax.dynamic_slice_in_dim(weights, column_start, width, 1)
    partial_value = jnp.dot(author_feat, local_weights[0], preferred_element_type=jnp.float32)
    partial_value = partial_value + jnp.dot(
        averages[0], local_weights[1], preferred_element_type=jnp.float32
    )
    refreshed = lax.psum_scatter(partial_value, "rep", scatter_dimension=1, tiled=True).astype(
        jnp.bfloat16
    )
    own_relation = lax.dynamic_slice_in_dim(relation, column_start, width, 0)
    queries = (jnp.take(refreshed, cand_author, axis=0).astype(jnp.float32) * own_relation).astype(
        jnp.bfloat16
    )
    neg_local = jnp.take(paper_feat, neg_rows[0], axis=0)
    negatives = lax.all_gather(neg_local, "owner", axis=0, tiled=True)
    positive = jnp.sum(queries.astype(jnp.float32) * cand_rows.astype(jnp.float32), axis=1)
    negative = jnp.dot(queries, negatives.T, preferred_element_type=jnp.float32)
    positive, negative = (
        lax.psum(positive.astype(jnp.bfloat16), "rep").astype(jnp.float32),
        lax.psum(negative.astype(jnp.bfloat16), "rep").astype(jnp.float32),
    )
    losses = jax.nn.softplus(-positive) + jnp.mean(jax.nn.softplus(negative), axis=1)
    return (refreshed, losses)


def solution(mesh):
    placed = (
        P("owner", "rep"),
        P("owner", "rep"),
        P(),
        P(),
        P("owner", None, None),
        P(None, None, "owner"),
        P(None, None, "owner"),
        P("owner"),
        P("owner", None, None),
        P("owner", None),
    )
    return jax.shard_map(
        per_device,
        mesh=mesh,
        in_specs=placed,
        out_specs=(P("owner", "rep"), P("owner")),
        check_vma=False,
    )
```

profile of v0, /device:TPU:0, one launch (start us, length us, event | category | flops | bytes accessed | tf_op | source)
XLA Modules:
  0.0 522.3 jit_solution(4444047207282968888)
XLA Ops:
  10.5 64.8 %gather_fusion = bf16[16384,192]{1,0:T(8,128)(2,1)} fusion(bf16[2048,192]{1,0:T(8,128)(2,1)S(1)} %copy.29, s32[16384]{0:T(1024)S(1)} %broadcast_clamp_fusion), kind=kCustom, calls=%fused_computation | custom fusion | bytes 12648448 | tf_op jit(solution)/shard_map/jit(_take)/gather | solution.py:37
  75.4 10.6 %copy.30 = bf16[32,512,192]{1,2,0:T(8,128)(2,1)} copy(bf16[32,512,192]{2,1,0:T(8,128)(2,1)} %bitcast.83) | data formatting | bytes 12582912 | tf_op jit(solution)/shard_map/jit(_take)/gather | solution.py:37
  86.0 6.1 %broadcast_select_fusion = bf16[32,512,192]{1,2,0:T(8,128)(2,1)} fusion(bf16[32,512,192]{1,2,0:T(8,128)(2,1)} %copy.30, pred[32,512]{1,0:T(8,128)(4,1)S(1)} %compare_and_fusion), kind=kLoop, calls=%fused_computation.26 | loop fusion | flops 3145728 | bytes 12599296 | tf_op jit(solution)/shard_map/jit(_take)/select_n | solution.py:37
  92.1 8.5 %all-to-all-start = ((bf16[32,512,192]{1,2,0:T(8,128)(2,1)}), bf16[32,512,192]{1,2,0:T(8,128)(2,1)}, u32[]{:S(2)}, u32[]{:S(2)}) async-start(bf16[32,512,192]{1,2,0:T(8,128)(2,1)} %broadcast_select_fusion), calls=%async_computation | async-start | bytes 12582912 | tf_op jit(solution)/shard_map/all_to_all | solution.py:40
  100.7 77.8 %all-to-all-done = bf16[32,512,192]{1,2,0:T(8,128)(2,1)} async-done(((bf16[32,512,192]{1,2,0:T(8,128)(2,1)}), bf16[32,512,192]{1,2,0:T(8,128)(2,1)}, u32[]{:S(2)}, u32[]{:S(2)}) %all-to-all-start) | async-done | bytes 6291488 | tf_op jit(solution)/shard_map/all_to_all | solution.py:40
  178.5 9.0 %copy.31 = bf16[32,512,192]{1,0,2:T(8,128)(2,1)} copy(bf16[32,512,192]{1,2,0:T(8,128)(2,1)} %all-to-all-done) | data formatting | bytes 12582912 | tf_op jit(solution)/shard_map/all_to_all | solution.py:40
  187.5 10.7 %reshape.169 = bf16[128,128,192]{1,0,2:T(8,128)(2,1)} reshape(bf16[32,512,192]{1,0,2:T(8,128)(2,1)} %copy.31) | data formatting | bytes 12582912 | tf_op jit(solution)/shard_map/reshape | solution.py:43
  198.2 172.6 %while.10 = (s32[]{:T(128)}, bf16[16,1,128,192]{2,3,1,0:T(8,128)(2,1)}, s32[16]{0:T(128)S(1)}, s32[1,48,2048]{2,1,0:T(8,128)}, s32[1,48,16]{1,2,0:T(8,128)}, /*i...) while((s32[]{:T(128)}, ...), condition=%wide.region_2.3_spmd, body=%wide.region_0.0_spmd.sunk | while | flops 606019584 | bytes 11160853 | solution.py:51
  203.3 3.8 convolution_convert_fusion.3
  214.1 3.8 convolution_convert_fusion.3
  224.9 3.8 convolution_convert_fusion.3
  235.7 3.8 convolution_convert_fusion.3
  246.5 3.8 convolution_convert_fusion.3
  257.3 3.8 convolution_convert_fusion.3
  268.1 3.8 convolution_convert_fusion.3
  278.8 3.8 convolution_convert_fusion.3
  289.6 3.8 convolution_convert_fusion.3
  300.4 3.8 convolution_convert_fusion.3
  311.2 3.8 convolution_convert_fusion.3
  322.0 3.8 convolution_convert_fusion.3
  332.8 3.8 convolution_convert_fusion.3
  343.6 3.8 convolution_convert_fusion.3
  354.4 3.8 convolution_convert_fusion.3
  378.9 24.7 %all_gather.3 = bf16[1024,192]{1,0:T(8,128)(2,1)} all-gather(bf16[32,192]{1,0:T(8,128)(2,1)S(1)} %broadcast_select_fusion.2), channel_id=1, replica_groups=mesh['owner'=32,'rep'=4] {'owner'}, dimensions={0}, use_global_device_ids=true | all-gather | bytes 405504 | tf_op jit(solution)/shard_map/all_gather | solution.py:66
  403.7 34.7 %reduce-scatter.2.cloned.1.call-done = f32[2048,192]{0,1:T(8,128)} async-done(((f32[2048,768]{0,1:T(8,128)}), f32[2048,192]{0,1:T(8,128)}) %reduce-scatter.2.cloned.1.call-update) | async-done | bytes 1572880 | tf_op jit(solution)/shard_map/reduce_scatter | solution.py:58
  443.0 6.0 %gather_fusion.1 = bf16[1024,192]{1,0:T(8,128)(2,1)} fusion(bf16[2048,192]{1,0:T(8,128)(2,1)} %copy.33, s32[1024]{0:T(1024)S(1)} %fusion.36), kind=kCustom, calls=%fused_computation.1 | custom fusion | bytes 790528 | tf_op jit(solution)/shard_map/jit(_take)/gather | solution.py:62
  452.3 4.9 gather_fusion.2
  459.3 7.3 %all-to-all-start.1 = ((bf16[32,32,192]{2,1,0:T(8,128)(2,1)}), bf16[32,32,192]{2,1,0:T(8,128)(2,1)S(1)}, u32[]{:S(2)}, u32[]{:S(2)}) async-start(bf16[32,32,192]{2,1,0:T(8,128)(2,1)} %broadcast_select_fusion.1), calls=%async_computation.2 | async-start | bytes 1048576 | tf_op jit(solution)/shard_map/all_to_all | solution.py:41
  466.7 11.7 %all-to-all-done.1 = bf16[32,32,192]{2,1,0:T(8,128)(2,1)S(1)} async-done(((bf16[32,32,192]{2,1,0:T(8,128)(2,1)}), bf16[32,32,192]{2,1,0:T(8,128)(2,1)S(1)}, u32[]{:S(2)}, u32[]{:S(2)}) %all-to-all-start.1) | async-done | bytes 393248 | tf_op jit(solution)/shard_map/all_to_all | solution.py:41
  480.0 8.6 %psum.14 = bf16[1024]{0:T(1024)(128)(2,1)S(1)} all-reduce(bf16[1024]{0:T(1024)(128)(2,1)S(1)} %convert_element_type.57), channel_id=1, replica_groups=mesh['owner'=32,'rep'=4] {'rep'}, use_global_device_ids=true, to_apply=%region_5.6 | all-reduce | flops 1024 | bytes 4096 | tf_op jit(solution)/shard_map/psum | solution.py:70
  488.5 22.2 %all-reduce.2.cloned.1.call-done = bf16[1024,1024]{1,0:T(8,128)(2,1)} async-done(((bf16[1024,1024]{1,0:T(8,128)(2,1)}), bf16[1024,1024]{1,0:T(8,128)(2,1)}) %all-reduce.2.cloned.1.call-update) | async-done | bytes 2097168 | tf_op jit(solution)/shard_map/psum | solution.py:71
  510.8 4.1 fusion.26
  (141 shorter events, 102.4 us)
Async XLA Ops:
  7.2 365.3 %copy-start = (bf16[2,768,768]{2,1,0:T(8,128)(2,1)S(1)}, bf16[2,768,768]{2,1,0:T(8,128)(2,1)}, u32[]{:S(2)}) copy-start(bf16[2,768,768]{2,1,0:T(8,128)(2,1)} %param.14) | copy-start | bytes 7077892
  92.1 86.4 %all-to-all-start = ((bf16[32,512,192]{1,2,0:T(8,128)(2,1)}), bf16[32,512,192]{1,2,0:T(8,128)(2,1)}, u32[]{:S(2)}, u32[]{:S(2)}) async-start(bf16[32,512,192]{1,2,0:T(8,128)(2,1)} %broadcast_select_fusion), calls=%async_computation | async-start | bytes 12582912 | tf_op jit(solution)/shard_map/all_to_all | solution.py:40
  100.6 337.7 %reduce-scatter.2.cloned.1.call-start = ((), (), s32[]{:S(2)}) async-start(), calls=%async_computation.3 | async-start | bytes 7864320 | tf_op jit(solution)/shard_map/reduce_scatter | solution.py:58
  372.5 1.1 copy-start.1
  377.3 0.8 copy-start.4
  377.3 26.3 %copy-start.3 = (s32[1024]{0:T(1024)S(1)}, s32[1024]{0:T(1024)}, u32[]{:S(2)}) copy-start(s32[1024]{0:T(1024)} %param.19) | copy-start | bytes 12292
  377.3 133.4 %all-reduce.2.cloned.1.call-start = ((), (), s32[]{:S(2)}) async-start(), calls=%async_computation.4 | async-start | bytes 4194304 | tf_op jit(solution)/shard_map/psum | solution.py:71
  443.0 9.3 %copy-start.2 = (s32[1,32,32]{2,1,0:T(8,128)S(1)}, s32[1,32,32]{2,1,0:T(8,128)}, u32[]{:S(2)}) copy-start(s32[1,32,32]{2,1,0:T(8,128)} %param.20) | copy-start | bytes 12292
  459.3 19.0 %all-to-all-start.1 = ((bf16[32,32,192]{2,1,0:T(8,128)(2,1)}), bf16[32,32,192]{2,1,0:T(8,128)(2,1)S(1)}, u32[]{:S(2)}, u32[]{:S(2)}) async-start(bf16[32,32,192]{2,1,0:T(8,128)(2,1)} %broadcast_select_fusion.1), calls=%async_computation.2 | async-start | bytes 1048576 | tf_op jit(solution)/shard_map/all_to_all | solution.py:41
Sparse Core Ops, SparseCore 0:
  377.5 60.8 reduce-scatter.1
  452.4 58.3 all-reduce.1
where the time goes:
time: 528 us; the launch traced here: 522 us
  local copies, waits for them, and re-layouts  146 us (28%)
  waiting for transfers between devices  146 us (28%)
  matrix products  98.9 us (19%)
  loops' own time  37.1 us (7%)
  blocking collectives  33.3 us (6%)
  other arithmetic  31 us (6%)
  starting transfers between devices  15.9 us (3%)
  between operations  14.2 us (3%)
    all_to_all x1, waiting for transfers between devices, per_device(): lax.all_to_all(outgoing, 'owner', split_axis=0, concat_axis=0, tiled=True)  77.8 us
    gather x2, local copies, waits for them, and re-layouts, per_device(): outgoing = jnp.take(paper_feat, send_rows[0], axis=0)  75.5 us
    dot_general x16, matrix products, block_means(): jnp.einsum('rtb,bjc->rtjc', selector, blocks, preferred_element_type=jnp....  60.6 us
    another operation x1, loops' own time, per_device(): lax.map(one_block, jnp.arange(tile_src.shape[2], dtype=jnp.int32))  37.1 us
    reduce_scatter x1, waiting for transfers between devices, per_device(): lax.psum_scatter(partial_value, 'rep', scatter_dimension=1, tiled=True)  34.7 us
    dot_general x16, matrix products, block_means(): jnp.einsum('rtij,rtjc->ric', one_hot, picked, preferred_element_type=jnp....  30.2 us
    all_gather x1, blocking collectives, per_device(): negatives = lax.all_gather(neg_local, 'owner', axis=0, tiled=True)  24.7 us
    psum x1, waiting for transfers between devices, per_device(): lax.psum(negative.astype(jnp.bfloat16), 'rep').astype(jnp.float32)  22.2 us
  transfers between devices with their start and end apart: 4, of which 4 were waited for; matrix products, arithmetic and copies ran while one was open for 2% of the time, Pallas kernels for 0%

commit v1 on v0

v1 whole, which is shorter than its diff:
```python
import jax
import jax.numpy as jnp
from jax import lax
from jax.experimental import pallas as pl
from jax.experimental.pallas import tpu as pltpu
from jax.sharding import PartitionSpec as P

MESH = pl.DeviceIdType.MESH
BF = jnp.bfloat16
F32 = jnp.float32
I32 = jnp.int32

W = 192
ROWS = 2048
CAP = 512
SLOTS = 48
D = 768


def iota(shape, dim):
    return lax.broadcasted_iota(I32, shape, dim)


def one_hot(rows, picks):
    return (iota((rows, picks.shape[1]), 0) == picks).astype(BF)


def kernel(
    src_ref,
    paper_ref,
    author_ref,
    weights_ref,
    relation_ref,
    idx_ref,
    col_ref,
    edge_ref,
    out_ref,
    loss_ref,
    paper_t,
    author_t,
    idx_all,
    send_buf,
    recv,
    cand_acc,
    neg_acc,
    cand_send,
    neg_send,
    cand_rx,
    cand_all,
    neg_all,
    neg_rows,
    weights_v,
    weights_t,
    relation_b,
    avg_all,
    self_part,
    self_sel,
    avg_sel,
    edge_hot,
    w_sem,
    p1_send,
    p1_recv,
    i1_send,
    i1_recv,
    au_send,
    au_recv,
    main_send,
    main_recv,
    cand_ssem,
    cand_rsem,
    neg_ssem,
    neg_rsem,
    nx_send,
    nx_recv,
    swap_send,
    swap_recv,
    cx_send,
    cx_recv,
    avg_ssem,
    avg_rsem,
    loss_ssem,
    loss_rsem,
):
    owner = lax.axis_index("owner")
    x = lax.axis_index("rep")
    core = owner % 2
    y = (owner // 2) % 4
    z = owner // 8
    even = 1 - core
    a = z * even + y * core
    b = y * even + z * core

    def owner_at(a_pos, b_pos, core_pos):
        return (a_pos * even + b_pos * core) * 8 + (b_pos * even + a_pos * core) * 2 + core_pos

    def device(da=0, db=0, dcore=0, dx=0):
        return {
            "owner": owner_at((a + da) % 4, (b + db) % 4, (core + dcore) % 2),
            "rep": (x + dx) % 4,
        }

    def remote(src, dst, ssem, rsem, target):
        return pltpu.make_async_remote_copy(
            src_ref=src,
            dst_ref=dst,
            send_sem=ssem,
            recv_sem=rsem,
            device_id=target,
            device_id_type=MESH,
        )

    barrier = pltpu.get_barrier_semaphore()
    partners = [device(da=k) for k in (1, 2, 3)] + [device(db=k) for k in (1, 2, 3)]
    partners += [device(da=k, dcore=1) for k in (0, 1, 2, 3)]
    partners += [device(db=k, dcore=1) for k in (1, 2, 3)]
    partners += [device(dx=k) for k in (1, 2, 3)]
    for partner in partners:
        pl.semaphore_signal(barrier, inc=1, device_id=partner, device_id_type=MESH)

    weights_copy = pltpu.make_async_copy(weights_ref, weights_v, w_sem)
    weights_copy.start()
    paper_t[0] = jnp.transpose(paper_ref[...])
    author_t[x] = jnp.transpose(author_ref[...])
    idx_all[0] = idx_ref[a]
    pl.semaphore_wait(barrier, len(partners))

    first = []
    for da in (1, 3, 2):
        slot = 4 - da
        first.append(
            remote(
                idx_ref.at[(a + da) % 4], idx_all.at[slot], i1_send.at[slot], i1_recv.at[slot], device(da=da)
            )
        )
        first.append(
            remote(paper_t.at[0], paper_t.at[slot], p1_send.at[slot], p1_recv.at[slot], device(da=da))
        )
    for copy in first:
        copy.start()
    authors = []
    for dx in (1, 3, 2):
        authors.append(
            remote(author_t.at[x], author_t.at[x], au_send.at[dx], au_recv.at[dx], device(dx=dx))
        )
    for copy in authors:
        copy.start()

    def main_copy(da, k):
        db = (k // 2 + 1) % 4
        dcore = k % 2
        source = owner_at((a + da) % 4, b, core)
        return remote(
            send_buf.at[da, k],
            recv.at[pl.ds(4 * source, 4)],
            main_send.at[da, k],
            main_recv.at[source],
            device(db=db, dcore=dcore),
        )

    def main_local(da, k):
        source = owner_at((a + da) % 4, b, core)
        return pltpu.make_async_copy(
            send_buf.at[da, k], recv.at[pl.ds(4 * source, 4)], main_recv.at[source]
        )

    def select_main(da):
        def step(k, carry):
            row = ((b + k // 2 + 1) % 4) * 2 + (core + k) % 2
            picks = idx_all[da, pl.ds(row, 1), :]
            out = jnp.dot(paper_t[da], one_hot(ROWS, picks), preferred_element_type=F32).astype(BF)
            for j in range(4):
                send_buf[da, k, j] = out[:, j * 128 : (j + 1) * 128]

            @pl.when(k == 6)
            def _():
                main_local(da, k).start()

            @pl.when(k != 6)
            def _():
                main_copy(da, k).start()

            return carry

        lax.fori_loop(0, 8, step, 0)

    group = iota((W, 128), 1) // 32

    def select_extra(da):
        a_src = (a + da) % 4
        picks = idx_all[da, 8:9, 0:384]
        out = jnp.dot(paper_t[da], one_hot(ROWS, picks), preferred_element_type=F32)
        here = group == a_src
        for d in range(8):
            part = out[:, (d // 4) * 128 : (d // 4 + 1) * 128]
            part = pltpu.roll(part, ((a_src + 4 - d % 4) % 4) * 32, 1)
            old = jnp.zeros((W, 128), F32) if da == 0 else cand_acc[d]
            cand_acc[d] = jnp.where(here, part, old)
        old = jnp.zeros((W, 128), F32) if da == 0 else neg_acc[...]
        neg_acc[...] = jnp.where(here, out[:, 256:384], old)

    def cand_copy(k):
        return remote(
            cand_send.at[((b + k // 2 + 1) % 4) * 2 + (core + k) % 2],
            cand_rx.at[b, core],
            cand_ssem.at[k],
            cand_rsem.at[b * 2 + core],
            device(db=(k // 2 + 1) % 4, dcore=k % 2),
        )

    def cand_local():
        return pltpu.make_async_copy(
            cand_send.at[b * 2 + core], cand_rx.at[b, core], cand_rsem.at[b * 2 + core]
        )

    def neg_copy(db):
        return remote(
            neg_send, neg_all.at[core, x, b], neg_ssem.at[db], neg_rsem.at[b], device(db=db)
        )

    def neg_local():
        return pltpu.make_async_copy(neg_send, neg_all.at[core, x, b], neg_rsem.at[b])

    select_main(0)
    select_extra(0)
    weights_copy.wait()
    for w in range(2):
        weights_t[w] = jnp.transpose(weights_v[w])
    for i in range(6):
        row = jnp.broadcast_to(relation_ref[i : i + 1, :], (128, 128))
        relation_b[pl.ds(i * 128, 128), :] = jnp.transpose(row)
    edge_hot[...] = one_hot(ROWS, edge_ref[...])

    def first_wait(slot):
        first_idx = remote(
            idx_ref.at[0], idx_all.at[slot], i1_send.at[slot], i1_recv.at[slot], device(da=1)
        )
        first_paper = remote(
            paper_t.at[0], paper_t.at[slot], p1_send.at[slot], p1_recv.at[slot], device(da=1)
        )
        first_idx.wait_recv()
        first_paper.wait_recv()

    first_wait(1)
    select_extra(1)
    select_main(1)
    first_wait(3)
    select_extra(3)
    first_wait(2)
    select_extra(2)
    for d in range(8):
        cand_send[d] = cand_acc[d].astype(BF)
    neg_send[...] = neg_acc[...].astype(BF)
    for db in (1, 3, 2):
        neg_copy(db).start()
    neg_local().start()
    for k in (0, 1, 2, 3, 4, 5, 7):
        cand_copy(k).start()
    cand_local().start()
    select_main(3)

    for slot in range(4):
        pltpu.make_async_copy(neg_send, neg_all.at[core, x, slot], neg_rsem.at[slot]).wait()
    neg_x = [
        remote(neg_all.at[core, x], neg_all.at[core, x], nx_send.at[dx], nx_recv.at[dx], device(dx=dx))
        for dx in (1, 3, 2)
    ]
    for copy in neg_x:
        copy.start()
    for slot in range(8):
        pltpu.make_async_copy(
            cand_send.at[0], cand_rx.at[slot // 2, slot % 2], cand_rsem.at[slot]
        ).wait()
    cand_x = [
        remote(
            cand_rx.at[(x + dx) % 4], cand_all.at[x], cx_send.at[dx], cx_recv.at[dx], device(dx=dx)
        )
        for dx in (1, 3, 2)
    ]
    for copy in cand_x:
        copy.start()
    cand_all[x] = cand_rx[x]
    select_main(2)

    for copy in neg_x:
        copy.wait_recv()
    swap = remote(neg_all.at[core], neg_all.at[core], swap_send, swap_recv, device(dcore=1))
    swap.start()

    for copy in authors:
        copy.wait_recv()
    own_rows = pl.ds(pl.multiple_of(x * W, 16), W)
    for g in range(4):
        lanes = pl.ds(g * 512, 512)
        block = jnp.concatenate([author_t[i, :, lanes] for i in range(4)], axis=0)
        self_part[:, lanes] = jnp.dot(weights_t[0, own_rows, :], block, preferred_element_type=F32)
    author_sel = [
        jnp.dot(author_t[i], edge_hot[...], preferred_element_type=F32).astype(BF) for i in range(4)
    ]
    self_sel[...] = jnp.dot(
        weights_t[0], jnp.concatenate(author_sel, axis=0), preferred_element_type=F32
    )
    swap.wait()
    for c in range(2):
        for i in range(4):
            block = jnp.concatenate([neg_all[c, j, i] for j in range(4)], axis=0)
            neg_rows[pl.ds((c * 4 + i) * 128, 128), :] = jnp.transpose(block)

    def recv_wait(s, carry):
        pltpu.make_async_copy(
            send_buf.at[0, 0], recv.at[pl.ds(4 * s, 4)], main_recv.at[s]
        ).wait()
        return carry

    lax.fori_loop(0, 32, recv_wait, 0)

    def avg_copy(g, dx):
        return remote(
            avg_all.at[x, g], avg_all.at[x, g], avg_ssem.at[g, dx], avg_rsem.at[g, dx], device(dx=dx)
        )

    def aggregate(block, carry):
        lanes = pl.ds(pl.multiple_of(block * 128, 128), 128)
        live = (col_ref[:, lanes] < 128).astype(F32)
        scale = 1.0 / jnp.maximum(jnp.sum(live, axis=0, keepdims=True), 1.0)
        total = jnp.zeros((W, 128), F32)
        for t in range(0, SLOTS, 8):
            left = [recv[src_ref[t + i, block]] for i in range(8)]
            right = [one_hot(128, col_ref[t + i : t + i + 1, lanes]) for i in range(8)]
            total = total + jnp.dot(
                jnp.concatenate(left, axis=1),
                jnp.concatenate(right, axis=0),
                preferred_element_type=F32,
            )
        g = block // 4
        inner = pl.ds(pl.multiple_of((block % 4) * 128, 128), 128)
        avg_all[x, g, :, inner] = (total * scale).astype(BF)

        @pl.when(block % 4 == 3)
        def _():
            for dx in (1, 3, 2):
                avg_copy(g, dx).start()

        return carry

    lax.fori_loop(0, 16, aggregate, 0)

    avg_sel[...] = jnp.zeros_like(avg_sel)

    def dense(g, carry):
        for dx in (1, 3, 2):
            avg_copy(g, dx).wait_recv()
        lanes = pl.ds(pl.multiple_of(g * 512, 512), 512)
        block = jnp.concatenate([avg_all[i, g] for i in range(4)], axis=0)
        mixed = self_part[:, lanes] + jnp.dot(
            weights_t[1, own_rows, :], block, preferred_element_type=F32
        )
        out_ref[:, lanes] = mixed.astype(BF)
        hot = edge_hot[pl.ds(pl.multiple_of(g * 512, 512), 512), :]
        avg_sel[...] += jnp.dot(block, hot, preferred_element_type=F32)
        return carry

    lax.fori_loop(0, 4, dense, 0)

    refreshed = self_sel[...] + jnp.dot(
        weights_t[1], avg_sel[...].astype(BF), preferred_element_type=F32
    )
    gain = jnp.concatenate([relation_b[...]] * 2, axis=1)
    queries = (refreshed.astype(BF).astype(F32) * gain).astype(BF)
    for copy in cand_x:
        copy.wait_recv()
    positive = jnp.zeros((1, 256), F32)
    for i in range(4):
        rows = jnp.concatenate([cand_all[i, 0], cand_all[i, 1]], axis=1).astype(F32)
        query = queries[i * W : (i + 1) * W].astype(F32)
        positive = positive + jnp.sum(query * rows, axis=0, keepdims=True)

    def softplus(v):
        return jnp.maximum(v, 0.0) + jnp.log1p(jnp.exp(-jnp.abs(v)))

    negative = jnp.dot(neg_rows[...], queries, preferred_element_type=F32)
    losses = softplus(-positive) + jnp.sum(softplus(negative), axis=0, keepdims=True) / 1024.0
    loss_ref[x, 0:1, :] = losses[:, 0:128]
    loss_ref[x, 1:2, :] = losses[:, 128:256]
    loss_copies = [
        remote(loss_ref.at[x], loss_ref.at[x], loss_ssem.at[dx], loss_rsem.at[dx], device(dx=dx))
        for dx in (1, 3, 2)
    ]
    for copy in loss_copies:
        copy.start()

    for copy in first + authors + neg_x + cand_x:
        copy.wait_send()
    for db in (1, 3, 2):
        neg_copy(db).wait_send()
    for k in (0, 1, 2, 3, 4, 5, 7):
        cand_copy(k).wait_send()

    def main_drain(k, carry):
        for da in range(4):

            @pl.when(k != 6)
            def _():
                main_copy(da, k).wait_send()

        return carry

    lax.fori_loop(0, 8, main_drain, 0)
    for g in range(4):
        for dx in (1, 3, 2):
            avg_copy(g, dx).wait_send()
    for copy in loss_copies:
        copy.wait()


def per_device(
    paper_feat,
    author_feat,
    weights,
    relation,
    send_rows,
    tile_src,
    tile_col,
    cand_author,
    cand_send,
    neg_rows,
):
    core = lax.axis_index("owner") % 2
    x = lax.axis_index("rep")

    def by_a(lists):
        lists = lists[0].reshape(4, 4, 2, -1)
        return jnp.where(core == 1, lists.transpose(1, 0, 2, 3), lists)

    rows = by_a(send_rows).reshape(4, 8, CAP)
    cands = by_a(cand_send).reshape(4, 1, 256)
    negs = jnp.broadcast_to(jnp.tile(neg_rows, (1, 4))[None], (4, 1, 128))
    last = jnp.concatenate([cands, negs, jnp.zeros((4, 1, 128), I32)], axis=2)
    idx = jnp.concatenate([rows, last, jnp.zeros((4, 7, CAP), I32)], axis=1)
    grid = cand_author.reshape(4, 4, 2, 32)
    first = lax.dynamic_index_in_dim(grid[:, :, 0], x, 1, keepdims=False).reshape(1, 128)
    second = lax.dynamic_index_in_dim(grid[:, :, 1], x, 0, keepdims=False).reshape(1, 128)
    edges = jnp.concatenate([first, second], axis=1)

    vmem = pl.BlockSpec(memory_space=pltpu.VMEM)
    dma = pltpu.SemaphoreType.DMA
    out, loss = pl.pallas_call(
        kernel,
        out_shape=(
            jax.ShapeDtypeStruct((W, ROWS), BF),
            jax.ShapeDtypeStruct((4, 8, 128), F32),
        ),
        in_specs=[
            pl.BlockSpec(memory_space=pltpu.SMEM),
            vmem,
            vmem,
            pl.BlockSpec(memory_space=pl.ANY),
            vmem,
            vmem,
            vmem,
            vmem,
        ],
        out_specs=(vmem, vmem),
        scratch_shapes=[
            pltpu.VMEM((4, W, ROWS), BF),
            pltpu.VMEM((4, W, ROWS), BF),
            pltpu.VMEM((4, 16, CAP), I32),
            pltpu.VMEM((4, 8, 4, W, 128), BF),
            pltpu.VMEM((128, W, 128), BF),
            pltpu.VMEM((8, W, 128), F32),
            pltpu.VMEM((W, 128), F32),
            pltpu.VMEM((8, W, 128), BF),
            pltpu.VMEM((W, 128), BF),
            pltpu.VMEM((4, 2, W, 128), BF),
            pltpu.VMEM((4, 2, W, 128), BF),
            pltpu.VMEM((2, 4, 4, W, 128), BF),
            pltpu.VMEM((1024, D), BF),
            pltpu.VMEM((2, D, D), BF),
            pltpu.VMEM((2, D, D), BF),
            pltpu.VMEM((D, 128), F32),
            pltpu.VMEM((4, 4, W, 512), BF),
            pltpu.VMEM((W, ROWS), F32),
            pltpu.VMEM((D, 256), F32),
            pltpu.VMEM((D, 256), F32),
            pltpu.VMEM((ROWS, 256), BF),
            dma,
            dma((4,)),
            dma((4,)),
            dma((4,)),
            dma((4,)),
            dma((4,)),
            dma((4,)),
            dma((4, 8)),
            dma((32,)),
            dma((8,)),
            dma((8,)),
            dma((4,)),
            dma((4,)),
            dma((4,)),
            dma((4,)),
            dma,
            dma,
            dma((4,)),
            dma((4,)),
            dma((4, 4)),
            dma((4, 4)),
            dma((4,)),
            dma((4,)),
        ],
        compiler_params=pltpu.CompilerParams(
            collective_id=0, has_side_effects=True, vmem_limit_bytes=60 * 2**20
        ),
        name="conv_and_score",
    )(
        tile_src[0],
        paper_feat,
        author_feat,
        weights,
        relation.reshape(6, 128),
        idx,
        tile_col[0],
        edges,
    )
    refreshed = out.T
    even = loss[:, 0].reshape(4, 4, 32).transpose(1, 0, 2)
    odd = loss[:, 1].reshape(4, 4, 32)
    return refreshed, jnp.stack([even, odd], axis=2).reshape(-1)


def solution(mesh):
    placed = (
        P("owner", "rep"),
        P("owner", "rep"),
        P(),
        P(),
        P("owner", None, None),
        P(None, None, "owner"),
        P(None, None, "owner"),
        P("owner"),
        P("owner", None, None),
        P("owner", None),
    )
    return jax.shard_map(
        per_device,
        mesh=mesh,
        in_specs=placed,
        out_specs=(P("owner", "rep"), P("owner")),
        check_vma=False,
    )
```

time: 528 us -> 131 us (0.25)
  waiting for transfers between devices: 146 us -> 0 us
  local copies, waits for them, and re-layouts: 146 us -> 11.6 us
  Pallas kernels: 0 us -> 115 us
  matrix products: 98.9 us -> 0 us
  loops' own time: 37.1 us -> 0 us
  blocking collectives: 33.3 us -> 0 us
  other arithmetic: 31 us -> 2.16 us
  starting transfers between devices: 15.9 us -> 0 us
  between operations: 14.2 us -> 0.73 us
    pallas_call x0 -> x1, Pallas kernels: none -> 115 us  [per_device(): pl.pallas_call(kernel, out_shape=(jax.ShapeDtypeStruct((W, ROWS), BF), ja...]
    dot_general x35 -> x0, matrix products: 98.9 us -> none  [the longest x16 60.6 us: block_means(): jnp.einsum('rtb,bjc->rtjc', selector, blocks, preferred_element_type=jnp....]
    all_to_all x2 -> x0, waiting for transfers between devices: 89.5 us -> none  [the longest x1 77.8 us: per_device(): lax.all_to_all(outgoing, 'owner', split_axis=0, concat_axis=0, tiled=True)]
    gather x5 -> x0, local copies, waits for them, and re-layouts: 87 us -> none  [the longest x2 75.5 us: per_device(): outgoing = jnp.take(paper_feat, send_rows[0], axis=0)]
    another operation x1 -> x0, loops' own time: 37.1 us -> none  [per_device(): lax.map(one_block, jnp.arange(tile_src.shape[2], dtype=jnp.int32))]
    reduce_scatter x1 -> x0, waiting for transfers between devices: 34.7 us -> none  [per_device(): lax.psum_scatter(partial_value, 'rep', scatter_dimension=1, tiled=True)]
    all_gather x1 -> x0, blocking collectives: 24.7 us -> none  [per_device(): negatives = lax.all_gather(neg_local, 'owner', axis=0, tiled=True)]
    eq x32 -> x0, local copies, waits for them, and re-layouts: 23.1 us -> none  [the longest x16 11.9 us: block_means(): columns[..., None] == jnp.arange(128, dtype=jnp.int32)]
  transfers between devices with their start and end apart: 4 -> 0, of which waited for: 4 -> 0; matrix products, arithmetic and copies ran while one was open for 2% -> 0% of each run, Pallas kernels for 0% -> 0%
where the time goes in v1:
time: 131 us; the launch traced here: 130 us
  Pallas kernels  115 us (88%)
  local copies, waits for them, and re-layouts  11.6 us (9%)
  other arithmetic  2.16 us (2%)
    pallas_call x1, Pallas kernels, per_device(): pl.pallas_call(kernel, out_shape=(jax.ShapeDtypeStruct((W, ROWS), BF), ja...  115 us
    unnamed x6, local copies, waits for them, and re-layouts  7.01 us

profile of v1, /device:TPU:0, one launch (start us, length us, event | category | flops | bytes accessed | tf_op | source)
XLA Modules:
  0.0 129.7 jit_solution(5203656817005653667)
XLA Ops:
  0.6 0.0 copy-start
  0.7 0.1 pad.8.clone
  0.7 0.7 tile.11
  1.4 0.1 reshape.68
  1.5 0.8 reshape.42
  2.4 0.1 reshape.44
  2.5 0.1 reshape.43
  2.5 0.6 pad_add_fusion.edge_ref
  3.1 0.8 copy_select_fusion.1
  3.9 0.1 reshape.41
  4.0 1.4 %copy.18 = s32[1,48,16]{2,1,0:T(8,128)} copy(s32[1,48,16]{1,2,0:T(8,128)} %param.15) | data formatting | bytes 6144 | tf_op args[5]
  5.4 0.9 reshape_squeeze.9
  6.4 0.7 add_add_fusion.idx_ref
  7.1 2.2 %copy.21.paper_ref = bf16[2048,192]{1,0:T(8,128)(2,1)} copy(bf16[2048,192]{0,1:T(8,128)(2,1)} %param.10) | data formatting | bytes 1572864 | tf_op args[0]
  9.4 0.0 copy-done
  9.4 1.3 %copy.22.author_ref = bf16[2048,192]{1,0:T(8,128)(2,1)} copy(bf16[2048,192]{0,1:T(8,128)(2,1)S(1)} %copy-done) | data formatting | bytes 1572864 | tf_op args[1]
  10.7 115.3 %conv_and_score.1 = (bf16[192,2048]{1,0:T(8,128)(2,1)}, f32[4,8,128]{2,1,0:T(8,128)}) custom-call(s32[48,16]{1,0:T(8,128)} %bitcast.17, bf16[2048,192]{1,0:T(8,128)(2,1)} %copy.21.paper_ref, bf16[2048,192]{1,0:T(8,128)(2,1)} %copy.22.author_ref, bf16[2,768,768]{2,1,0:T(8,128)(2,1)} %weights_ref.1, f32[6,128]{1,0:T(8,128)} %bitcast.22, ...), custom_call_target="tpu_custom_call" | custom-call | tf_op jit(solution)/shard_map/conv_and_score/pallas_call | solution.py:446
  126.0 0.8 slice_reduce_fusion.1
  126.8 0.1 reshape_squeeze.11
  126.9 0.1 stack_reshape_squeeze.3
  127.0 0.7 reshape.45
  127.7 2.1 %copy.28 = bf16[2048,192]{0,1:T(8,128)(2,1)} copy(bf16[2048,192]{0,1:T(8,128)(2,1)} %bitcast.15) | data formatting | bytes 1572864
  (11 shorter events, 0.2 us)
Async XLA Ops:
  0.6 8.7 %copy-start = (bf16[2048,192]{0,1:T(8,128)(2,1)S(1)}, bf16[2048,192]{0,1:T(8,128)(2,1)}, u32[]{:S(2)}) copy-start(bf16[2048,192]{0,1:T(8,128)(2,1)} %param.11) | copy-start | bytes 2359300

commit v2 on v1

--- a/solution.py
+++ b/solution.py
@@ -13,6 +13,7 @@
 W = 192
 ROWS = 2048
 CAP = 512
+HALF = 96
 SLOTS = 48
 D = 768
 
@@ -40,7 +41,8 @@
     author_t,
     idx_all,
     send_buf,
-    recv,
+    recv_first,
+    recv_second,
     cand_acc,
     neg_acc,
     cand_send,
@@ -60,10 +62,14 @@
     w_sem,
     p1_send,
     p1_recv,
+    f1_send,
+    f1_recv,
     i1_send,
     i1_recv,
     au_send,
     au_recv,
+    fa_send,
+    fa_recv,
     main_send,
     main_recv,
     cand_ssem,
@@ -78,9 +84,12 @@
     cx_recv,
     avg_ssem,
     avg_rsem,
+    fw_ssem,
+    fw_rsem,
     loss_ssem,
     loss_rsem,
 ):
+    recv = (recv_first, recv_second)
     owner = lax.axis_index("owner")
     x = lax.axis_index("rep")
     core = owner % 2
@@ -124,61 +133,78 @@
     idx_all[0] = idx_ref[a]
     pl.semaphore_wait(barrier, len(partners))
 
-    first = []
+    def row_list(da):
+        slot = 4 - da
+        return remote(
+            idx_ref.at[(a + da) % 4], idx_all.at[slot], i1_send.at[slot], i1_recv.at[slot], device(da=da)
+        )
+
+    def paper_copy(da):
+        slot = 4 - da
+        return remote(
+            paper_t.at[0], paper_t.at[slot], p1_send.at[slot], p1_recv.at[slot], device(da=da)
+        )
+
+    def half_of(way):
+        return pl.ds(0 if way == 1 else HALF, HALF)
+
+    def paper_forward(da):
+        slot = 4 - da
+        return remote(
+            paper_t.at[slot, half_of(da)],
+            paper_t.at[2, half_of(da)],
+            f1_send.at[slot],
+            f1_recv.at[slot],
+            device(da=da),
+        )
+
+    def author_copy(dx):
+        return remote(author_t.at[x], author_t.at[x], au_send.at[dx], au_recv.at[dx], device(dx=dx))
+
+    def author_forward(dx):
+        part = author_t.at[(x + 4 - dx) % 4, half_of(dx)]
+        return remote(part, part, fa_send.at[dx], fa_recv.at[dx], device(dx=dx))
+
     for da in (1, 3, 2):
-        slot = 4 - da
-        first.append(
-            remote(
-                idx_ref.at[(a + da) % 4], idx_all.at[slot], i1_send.at[slot], i1_recv.at[slot], device(da=da)
-            )
-        )
-        first.append(
-            remote(paper_t.at[0], paper_t.at[slot], p1_send.at[slot], p1_recv.at[slot], device(da=da))
-        )
-    for copy in first:
-        copy.start()
-    authors = []
-    for dx in (1, 3, 2):
-        authors.append(
-            remote(author_t.at[x], author_t.at[x], au_send.at[dx], au_recv.at[dx], device(dx=dx))
-        )
-    for copy in authors:
-        copy.start()
-
-    def main_copy(da, k):
+        row_list(da).start()
+    for da in (1, 3):
+        paper_copy(da).start()
+    for dx in (1, 3):
+        author_copy(dx).start()
+
+    def main_copy(da, k, h):
         db = (k // 2 + 1) % 4
         dcore = k % 2
         source = owner_at((a + da) % 4, b, core)
         return remote(
-            send_buf.at[da, k],
-            recv.at[pl.ds(4 * source, 4)],
-            main_send.at[da, k],
-            main_recv.at[source],
+            send_buf.at[da, k, h],
+            recv[h].at[pl.ds(4 * source, 4)],
+            main_send.at[h, da, k],
+            main_recv.at[h, source],
             device(db=db, dcore=dcore),
         )
 
-    def main_local(da, k):
-        source = owner_at((a + da) % 4, b, core)
-        return pltpu.make_async_copy(
-            send_buf.at[da, k], recv.at[pl.ds(4 * source, 4)], main_recv.at[source]
-        )
+    def main_start(da, k, h):
+        @pl.when(k == 6)
+        def _():
+            source = owner_at((a + da) % 4, b, core)
+            pltpu.make_async_copy(
+                send_buf.at[da, k, h], recv[h].at[pl.ds(4 * source, 4)], main_recv.at[h, source]
+            ).start()
+
+        @pl.when(k != 6)
+        def _():
+            main_copy(da, k, h).start()
 
     def select_main(da):
         def step(k, carry):
             row = ((b + k // 2 + 1) % 4) * 2 + (core + k) % 2
             picks = idx_all[da, pl.ds(row, 1), :]
             out = jnp.dot(paper_t[da], one_hot(ROWS, picks), preferred_element_type=F32).astype(BF)
-            for j in range(4):
-                send_buf[da, k, j] = out[:, j * 128 : (j + 1) * 128]
-
-            @pl.when(k == 6)
-            def _():
-                main_local(da, k).start()
-
-            @pl.when(k != 6)
-            def _():
-                main_copy(da, k).start()
-
+            for h in range(2):
+                for j in range(4):
+                    send_buf[da, k, h, j] = out[h * HALF : (h + 1) * HALF, j * 128 : (j + 1) * 128]
+            main_start(da, k, 0)
             return carry
 
         lax.fori_loop(0, 8, step, 0)
@@ -224,28 +250,29 @@
     select_extra(0)
     weights_copy.wait()
     for w in range(2):
-        weights_t[w] = jnp.transpose(weights_v[w])
+        for h in range(2):
+            rows = [weights_v[w, pl.ds(i * W + h * HALF, HALF), :] for i in range(4)]
+            weights_t[w, h] = jnp.transpose(jnp.concatenate(rows, axis=0))
     for i in range(6):
         row = jnp.broadcast_to(relation_ref[i : i + 1, :], (128, 128))
         relation_b[pl.ds(i * 128, 128), :] = jnp.transpose(row)
     edge_hot[...] = one_hot(ROWS, edge_ref[...])
 
-    def first_wait(slot):
-        first_idx = remote(
-            idx_ref.at[0], idx_all.at[slot], i1_send.at[slot], i1_recv.at[slot], device(da=1)
-        )
-        first_paper = remote(
-            paper_t.at[0], paper_t.at[slot], p1_send.at[slot], p1_recv.at[slot], device(da=1)
-        )
-        first_idx.wait_recv()
-        first_paper.wait_recv()
-
-    first_wait(1)
+    for da in (1, 3):
+        paper_copy(da).wait_recv()
+        paper_forward(da).start()
+    row_list(3).wait_recv()
+    select_main(1)
     select_extra(1)
-    select_main(1)
-    first_wait(3)
+    row_list(1).wait_recv()
+    select_main(3)
     select_extra(3)
-    first_wait(2)
+    for dx in (1, 3):
+        author_copy(dx).wait_recv()
+        author_forward(dx).start()
+    row_list(2).wait_recv()
+    for da in (1, 3):
+        paper_forward(da).wait_recv()
     select_extra(2)
     for d in range(8):
         cand_send[d] = cand_acc[d].astype(BF)
@@ -256,7 +283,14 @@
     for k in (0, 1, 2, 3, 4, 5, 7):
         cand_copy(k).start()
     cand_local().start()
-    select_main(3)
+    select_main(2)
+
+    def second_half(k, carry):
+        for da in (0, 1, 3, 2):
+            main_start(da, k, 1)
+        return carry
+
+    lax.fori_loop(0, 8, second_half, 0)
 
     for slot in range(4):
         pltpu.make_async_copy(neg_send, neg_all.at[core, x, slot], neg_rsem.at[slot]).wait()
@@ -279,91 +313,128 @@
     for copy in cand_x:
         copy.start()
     cand_all[x] = cand_rx[x]
-    select_main(2)
-
+
+    def avg_copy(h, g, dx):
+        part = avg_all.at[h, x, g]
+        return remote(part, part, avg_ssem.at[h, g, dx], avg_rsem.at[h, g, dx], device(dx=dx))
+
+    def avg_forward(h, g, dx):
+        part = avg_all.at[h, (x + 4 - dx) % 4, g, pl.ds(0 if dx == 1 else HALF // 2, HALF // 2)]
+        return remote(part, part, fw_ssem.at[h, g, dx], fw_rsem.at[h, g, dx], device(dx=dx))
+
+    def pass_on(h, g):
+        for dx in (1, 3):
+            avg_copy(h, g, dx).wait_recv()
+            avg_forward(h, g, dx).start()
+
+    def aggregate(h):
+        def recv_wait(s, carry):
+            pltpu.make_async_copy(
+                send_buf.at[0, 0, h], recv[h].at[pl.ds(4 * s, 4)], main_recv.at[h, s]
+            ).wait()
+            return carry
+
+        lax.fori_loop(0, 32, recv_wait, 0)
+
+        def step(block, carry):
+            lanes = pl.ds(pl.multiple_of(block * 128, 128), 128)
+            live = (col_ref[:, lanes] < 128).astype(F32)
+            scale = 1.0 / jnp.maximum(jnp.sum(live, axis=0, keepdims=True), 1.0)
+            total = jnp.zeros((HALF, 128), F32)
+            for t in range(0, SLOTS, 8):
+                left = [recv[h][src_ref[t + i, block]] for i in range(8)]
+                right = [one_hot(128, col_ref[t + i : t + i + 1, lanes]) for i in range(8)]
+                total = total + jnp.dot(
+                    jnp.concatenate(left, axis=1),
+                    jnp.concatenate(right, axis=0),
+                    preferred_element_type=F32,
+                )
+            g = block // 4
+            inner = pl.ds(pl.multiple_of((block % 4) * 128, 128), 128)
+            avg_all[h, x, g, :, inner] = (total * scale).astype(BF)
+
+            @pl.when(block % 4 == 3)
+            def _():
+                for dx in (1, 3):
+                    avg_copy(h, g, dx).start()
+
+            @pl.when(block % 4 == 3)
+            def _():
+                @pl.when(g >= 2)
+                def _():
+                    pass_on(h, g - 2)
+
+            return carry
+
+        lax.fori_loop(0, 16, step, 0)
+
+    aggregate(0)
+
+    own_rows = pl.ds(pl.multiple_of(x * W, 16), W)
+    pass_on(0, 2)
+    for dx in (1, 3):
+        author_forward(dx).wait_recv()
+    for g in range(4):
+        lanes = pl.ds(g * 512, 512)
+        total = jnp.zeros((W, 512), F32)
+        for h in range(2):
+            block = [author_t[i, pl.ds(h * HALF, HALF), lanes] for i in range(4)]
+            total = total + jnp.dot(
+                weights_t[0, h, own_rows, :],
+                jnp.concatenate(block, axis=0),
+                preferred_element_type=F32,
+            )
+        self_part[:, lanes] = total
+    pass_on(0, 3)
+    author_sel = [
+        jnp.dot(author_t[i], edge_hot[...], preferred_element_type=F32).astype(BF) for i in range(4)
+    ]
+    total = jnp.zeros((D, 256), F32)
+    for h in range(2):
+        block = [author_sel[i][h * HALF : (h + 1) * HALF] for i in range(4)]
+        total = total + jnp.dot(
+            weights_t[0, h], jnp.concatenate(block, axis=0), preferred_element_type=F32
+        )
+    self_sel[...] = total
     for copy in neg_x:
         copy.wait_recv()
     swap = remote(neg_all.at[core], neg_all.at[core], swap_send, swap_recv, device(dcore=1))
     swap.start()
-
-    for copy in authors:
-        copy.wait_recv()
-    own_rows = pl.ds(pl.multiple_of(x * W, 16), W)
-    for g in range(4):
-        lanes = pl.ds(g * 512, 512)
-        block = jnp.concatenate([author_t[i, :, lanes] for i in range(4)], axis=0)
-        self_part[:, lanes] = jnp.dot(weights_t[0, own_rows, :], block, preferred_element_type=F32)
-    author_sel = [
-        jnp.dot(author_t[i], edge_hot[...], preferred_element_type=F32).astype(BF) for i in range(4)
-    ]
-    self_sel[...] = jnp.dot(
-        weights_t[0], jnp.concatenate(author_sel, axis=0), preferred_element_type=F32
-    )
     swap.wait()
     for c in range(2):
         for i in range(4):
             block = jnp.concatenate([neg_all[c, j, i] for j in range(4)], axis=0)
             neg_rows[pl.ds((c * 4 + i) * 128, 128), :] = jnp.transpose(block)
 
-    def recv_wait(s, carry):
-        pltpu.make_async_copy(
-            send_buf.at[0, 0], recv.at[pl.ds(4 * s, 4)], main_recv.at[s]
-        ).wait()
-        return carry
-
-    lax.fori_loop(0, 32, recv_wait, 0)
-
-    def avg_copy(g, dx):
-        return remote(
-            avg_all.at[x, g], avg_all.at[x, g], avg_ssem.at[g, dx], avg_rsem.at[g, dx], device(dx=dx)
-        )
-
-    def aggregate(block, carry):
-        lanes = pl.ds(pl.multiple_of(block * 128, 128), 128)
-        live = (col_ref[:, lanes] < 128).astype(F32)
-        scale = 1.0 / jnp.maximum(jnp.sum(live, axis=0, keepdims=True), 1.0)
-        total = jnp.zeros((W, 128), F32)
-        for t in range(0, SLOTS, 8):
-            left = [recv[src_ref[t + i, block]] for i in range(8)]
-            right = [one_hot(128, col_ref[t + i : t + i + 1, lanes]) for i in range(8)]
-            total = total + jnp.dot(
-                jnp.concatenate(left, axis=1),
-                jnp.concatenate(right, axis=0),
-                preferred_element_type=F32,
+    aggregate(1)
+    pass_on(1, 2)
+
+    def dense(h):
+        avg_sel[...] = jnp.zeros_like(avg_sel)
+
+        def step(g, carry):
+            for dx in (1, 3):
+                avg_forward(h, g, dx).wait_recv()
+            lanes = pl.ds(pl.multiple_of(g * 512, 512), 512)
+            block = jnp.concatenate([avg_all[h, i, g] for i in range(4)], axis=0)
+            mixed = self_part[:, lanes] + jnp.dot(
+                weights_t[1, h, own_rows, :], block, preferred_element_type=F32
             )
-        g = block // 4
-        inner = pl.ds(pl.multiple_of((block % 4) * 128, 128), 128)
-        avg_all[x, g, :, inner] = (total * scale).astype(BF)
-
-        @pl.when(block % 4 == 3)
-        def _():
-            for dx in (1, 3, 2):
-                avg_copy(g, dx).start()
-
-        return carry
-
-    lax.fori_loop(0, 16, aggregate, 0)
-
-    avg_sel[...] = jnp.zeros_like(avg_sel)
-
-    def dense(g, carry):
-        for dx in (1, 3, 2):
-            avg_copy(g, dx).wait_recv()
-        lanes = pl.ds(pl.multiple_of(g * 512, 512), 512)
-        block = jnp.concatenate([avg_all[i, g] for i in range(4)], axis=0)
-        mixed = self_part[:, lanes] + jnp.dot(
-            weights_t[1, own_rows, :], block, preferred_element_type=F32
-        )
-        out_ref[:, lanes] = mixed.astype(BF)
-        hot = edge_hot[pl.ds(pl.multiple_of(g * 512, 512), 512), :]
-        avg_sel[...] += jnp.dot(block, hot, preferred_element_type=F32)
-        return carry
-
-    lax.fori_loop(0, 4, dense, 0)
-
-    refreshed = self_sel[...] + jnp.dot(
-        weights_t[1], avg_sel[...].astype(BF), preferred_element_type=F32
-    )
+            if h == 0:
+                self_part[:, lanes] = mixed
+            else:
+                out_ref[:, lanes] = mixed.astype(BF)
+            hot = edge_hot[pl.ds(pl.multiple_of(g * 512, 512), 512), :]
+            avg_sel[...] += jnp.dot(block, hot, preferred_element_type=F32)
+            return carry
+
+        lax.fori_loop(0, 4, step, 0)
+        return jnp.dot(weights_t[1, h], avg_sel[...].astype(BF), preferred_element_type=F32)
+
+    self_sel[...] += dense(0)
+    pass_on(1, 3)
+    refreshed = self_sel[...] + dense(1)
+
     gain = jnp.concatenate([relation_b[...]] * 2, axis=1)
     queries = (refreshed.astype(BF).astype(F32) * gain).astype(BF)
     for copy in cand_x:
@@ -388,7 +459,14 @@
     for copy in loss_copies:
         copy.start()
 
-    for copy in first + authors + neg_x + cand_x:
+    for da in (1, 3, 2):
+        row_list(da).wait_send()
+    for way in (1, 3):
+        paper_copy(way).wait_send()
+        paper_forward(way).wait_send()
+        author_copy(way).wait_send()
+        author_forward(way).wait_send()
+    for copy in neg_x + cand_x:
         copy.wait_send()
     for db in (1, 3, 2):
         neg_copy(db).wait_send()
@@ -396,18 +474,24 @@
         cand_copy(k).wait_send()
 
     def main_drain(k, carry):
-        for da in range(4):
-
-            @pl.when(k != 6)
-            def _():
-                main_copy(da, k).wait_send()
+        @pl.when(k != 6)
+        def _():
+            for h in range(2):
+                for da in range(4):
+                    main_copy(da, k, h).wait_send()
 
         return carry
 
     lax.fori_loop(0, 8, main_drain, 0)
-    for g in range(4):
-        for dx in (1, 3, 2):
-            avg_copy(g, dx).wait_send()
+
+    def avg_drain(g, carry):
+        for h in range(2):
+            for dx in (1, 3):
+                avg_copy(h, g, dx).wait_send()
+                avg_forward(h, g, dx).wait_send()
+        return carry
+
+    lax.fori_loop(0, 4, avg_drain, 0)
     for copy in loss_copies:
         copy.wait()
 
@@ -464,8 +548,9 @@
             pltpu.VMEM((4, W, ROWS), BF),
             pltpu.VMEM((4, W, ROWS), BF),
             pltpu.VMEM((4, 16, CAP), I32),
-            pltpu.VMEM((4, 8, 4, W, 128), BF),
-            pltpu.VMEM((128, W, 128), BF),
+            pltpu.VMEM((4, 8, 2, 4, HALF, 128), BF),
+            pltpu.VMEM((128, HALF, 128), BF),
+            pltpu.VMEM((128, HALF, 128), BF),
             pltpu.VMEM((8, W, 128), F32),
             pltpu.VMEM((W, 128), F32),
             pltpu.VMEM((8, W, 128), BF),
@@ -475,12 +560,12 @@
             pltpu.VMEM((2, 4, 4, W, 128), BF),
             pltpu.VMEM((1024, D), BF),
             pltpu.VMEM((2, D, D), BF),
-            pltpu.VMEM((2, D, D), BF),
+            pltpu.VMEM((2, 2, D, D // 2), BF),
             pltpu.VMEM((D, 128), F32),
-            pltpu.VMEM((4, 4, W, 512), BF),
+            pltpu.VMEM((2, 4, 4, HALF, 512), BF),
             pltpu.VMEM((W, ROWS), F32),
             pltpu.VMEM((D, 256), F32),
-            pltpu.VMEM((D, 256), F32),
+            pltpu.VMEM((D // 2, 256), F32),
             pltpu.VMEM((ROWS, 256), BF),
             dma,
             dma((4,)),
@@ -489,8 +574,12 @@
             dma((4,)),
             dma((4,)),
             dma((4,)),
-            dma((4, 8)),
-            dma((32,)),
+            dma((4,)),
+            dma((4,)),
+            dma((4,)),
+            dma((4,)),
+            dma((2, 4, 8)),
+            dma((2, 32)),
             dma((8,)),
             dma((8,)),
             dma((4,)),
@@ -501,8 +590,10 @@
             dma,
             dma((4,)),
             dma((4,)),
-            dma((4, 4)),
-            dma((4, 4)),
+            dma((2, 4, 4)),
+            dma((2, 4, 4)),
+            dma((2, 4, 4)),
+            dma((2, 4, 4)),
             dma((4,)),
             dma((4,)),
         ],

time: 131 us -> 117 us (0.89)
  Pallas kernels: 115 us -> 102 us
    pallas_call x1, Pallas kernels: 115 us -> 102 us  [per_device(): pl.pallas_call(kernel, out_shape=(jax.ShapeDtypeStruct((W, ROWS), BF), ja...]
where the time goes in v2:
time: 117 us
  Pallas kernels  102 us (87%)
  local copies, waits for them, and re-layouts  11.6 us (10%)
  other arithmetic  2.16 us (2%)
    pallas_call x1, Pallas kernels, per_device(): pl.pallas_call(kernel, out_shape=(jax.ShapeDtypeStruct((W, ROWS), BF), ja...  102 us
    unnamed x6, local copies, waits for them, and re-layouts  7.01 us

profile of v2, /device:TPU:0, one launch (start us, length us, event | category | flops | bytes accessed | tf_op | source)
XLA Modules:
  0.0 116.7 jit_solution(7278144043584397184)
XLA Ops:
  0.6 0.0 copy-start
  0.7 0.1 pad.8.clone
  0.7 0.7 tile.11
  1.4 0.1 reshape.68
  1.5 0.8 reshape.42
  2.4 0.1 reshape.44
  2.5 0.1 reshape.43
  2.5 0.6 pad_add_fusion.edge_ref
  3.1 0.8 copy_select_fusion.1
  3.9 0.1 reshape.41
  4.0 1.4 %copy.18 = s32[1,48,16]{2,1,0:T(8,128)} copy(s32[1,48,16]{1,2,0:T(8,128)} %param.15) | data formatting | bytes 6144 | tf_op args[5]
  5.4 0.9 reshape_squeeze.9
  6.4 0.7 add_add_fusion.idx_ref
  7.1 2.2 %copy.21.paper_ref = bf16[2048,192]{1,0:T(8,128)(2,1)} copy(bf16[2048,192]{0,1:T(8,128)(2,1)} %param.10) | data formatting | bytes 1572864 | tf_op args[0]
  9.4 0.0 copy-done
  9.4 1.3 %copy.22.author_ref = bf16[2048,192]{1,0:T(8,128)(2,1)} copy(bf16[2048,192]{0,1:T(8,128)(2,1)S(1)} %copy-done) | data formatting | bytes 1572864 | tf_op args[1]
  10.7 102.2 %conv_and_score.1 = (bf16[192,2048]{1,0:T(8,128)(2,1)}, f32[4,8,128]{2,1,0:T(8,128)}) custom-call(s32[48,16]{1,0:T(8,128)} %bitcast.17, bf16[2048,192]{1,0:T(8,128)(2,1)} %copy.21.paper_ref, bf16[2048,192]{1,0:T(8,128)(2,1)} %copy.22.author_ref, bf16[2,768,768]{2,1,0:T(8,128)(2,1)} %weights_ref.1, f32[6,128]{1,0:T(8,128)} %bitcast.22, ...), custom_call_target="tpu_custom_call" | custom-call | tf_op jit(solution)/shard_map/conv_and_score/pallas_call | solution.py:530
  112.9 0.8 slice_reduce_fusion.1
  113.7 0.1 reshape_squeeze.11
  113.8 0.1 stack_reshape_squeeze.3
  113.9 0.7 reshape.45
  114.6 2.1 %copy.28 = bf16[2048,192]{0,1:T(8,128)(2,1)} copy(bf16[2048,192]{0,1:T(8,128)(2,1)} %bitcast.15) | data formatting | bytes 1572864
  (11 shorter events, 0.2 us)
Async XLA Ops:
  0.6 8.7 %copy-start = (bf16[2048,192]{0,1:T(8,128)(2,1)S(1)}, bf16[2048,192]{0,1:T(8,128)(2,1)}, u32[]{:S(2)}) copy-start(bf16[2048,192]{0,1:T(8,128)(2,1)} %param.11) | copy-start | bytes 2359300

commit v3 on v2

--- a/solution.py
+++ b/solution.py
@@ -31,11 +31,17 @@
     paper_ref,
     author_ref,
     weights_ref,
+    col_hbm,
     relation_ref,
-    idx_ref,
-    col_ref,
+    rows_ref,
+    cand_ref,
+    neg_ref,
     edge_ref,
     out_ref,
+    loss_out,
+    col_ref,
+    idx_ref,
+    tiled,
     loss_ref,
     paper_t,
     author_t,
@@ -60,6 +66,7 @@
     avg_sel,
     edge_hot,
     w_sem,
+    in_sem,
     p1_send,
     p1_recv,
     f1_send,
@@ -118,6 +125,15 @@
             device_id_type=MESH,
         )
 
+    paper_in = pltpu.make_async_copy(paper_ref, paper_t.at[0], in_sem.at[0])
+    author_in = pltpu.make_async_copy(author_ref, author_t.at[x], in_sem.at[1])
+    col_in = pltpu.make_async_copy(col_hbm, col_ref, in_sem.at[2])
+    weights_copy = pltpu.make_async_copy(weights_ref, weights_v, w_sem)
+    paper_in.start()
+    author_in.start()
+    weights_copy.start()
+    col_in.start()
+
     barrier = pltpu.get_barrier_semaphore()
     partners = [device(da=k) for k in (1, 2, 3)] + [device(db=k) for k in (1, 2, 3)]
     partners += [device(da=k, dcore=1) for k in (0, 1, 2, 3)]
@@ -126,11 +142,32 @@
     for partner in partners:
         pl.semaphore_signal(barrier, inc=1, device_id=partner, device_id_type=MESH)
 
-    weights_copy = pltpu.make_async_copy(weights_ref, weights_v, w_sem)
-    weights_copy.start()
-    paper_t[0] = jnp.transpose(paper_ref[...])
-    author_t[x] = jnp.transpose(author_ref[...])
+    lane_group = iota((1, 128), 1) // 32
+    place = (iota((32, 128), 1) % 32 == iota((32, 128), 0)).astype(BF)
+
+    def repeat_lanes(values):
+        high = (values // 64).astype(F32).astype(BF)
+        low = (values % 64).astype(F32).astype(BF)
+        high = jnp.dot(high, place, preferred_element_type=F32)
+        low = jnp.dot(low, place, preferred_element_type=F32)
+        return (high * 64.0 + low).astype(I32)
+
+    tiled[...] = repeat_lanes(cand_ref[...])
+    neg_row = repeat_lanes(jnp.broadcast_to(neg_ref[...], (8, 32)))[0:1]
+    for ap in range(4):
+        for d in range(8):
+            row = owner_at(ap, d // 2, d % 2)
+            idx_ref[ap, d : d + 1, :] = rows_ref[pl.ds(row, 1), :]
+        for j in range(2):
+            line = jnp.zeros((1, 128), I32)
+            for i in range(4):
+                row = tiled[pl.ds(owner_at(ap, 2 * j + i // 2, i % 2), 1), :]
+                line = jnp.where(lane_group == i, row, line)
+            idx_ref[ap, 8:9, j * 128 : (j + 1) * 128] = line
+        idx_ref[ap, 8:9, 256:384] = neg_row
     idx_all[0] = idx_ref[a]
+
+    paper_in.wait()
     pl.semaphore_wait(barrier, len(partners))
 
     def row_list(da):
@@ -169,6 +206,7 @@
         row_list(da).start()
     for da in (1, 3):
         paper_copy(da).start()
+    author_in.wait()
     for dx in (1, 3):
         author_copy(dx).start()
 
@@ -256,7 +294,16 @@
     for i in range(6):
         row = jnp.broadcast_to(relation_ref[i : i + 1, :], (128, 128))
         relation_b[pl.ds(i * 128, 128), :] = jnp.transpose(row)
-    edge_hot[...] = one_hot(ROWS, edge_ref[...])
+    halves = [jnp.zeros((8, 128), I32) for _ in range(2)]
+    for i in range(4):
+        row = jnp.broadcast_to(edge_ref[pl.ds(i * 2 + x // 2, 1), :], (8, 128))
+        row = pltpu.roll(row, ((i + 4 - (x % 2) * 2) % 4) * 32, 1)
+        halves[0] = jnp.where(lane_group == i, row, halves[0])
+        row = jnp.broadcast_to(edge_ref[pl.ds(x * 2 + i // 2, 1), :], (8, 128))
+        row = pltpu.roll(row, ((i + 3 - (i % 2) * 2) % 4) * 32, 1)
+        halves[1] = jnp.where(lane_group == i, row, halves[1])
+    edge_hot[...] = one_hot(ROWS, jnp.concatenate(halves, axis=1)[0:1])
+    col_in.wait()
 
     for da in (1, 3):
         paper_copy(da).wait_recv()
@@ -342,7 +389,7 @@
             scale = 1.0 / jnp.maximum(jnp.sum(live, axis=0, keepdims=True), 1.0)
             total = jnp.zeros((HALF, 128), F32)
             for t in range(0, SLOTS, 8):
-                left = [recv[h][src_ref[t + i, block]] for i in range(8)]
+                left = [recv[h][src_ref[block, t + i]] for i in range(8)]
                 right = [one_hot(128, col_ref[t + i : t + i + 1, lanes]) for i in range(8)]
                 total = total + jnp.dot(
                     jnp.concatenate(left, axis=1),
@@ -494,6 +541,15 @@
     lax.fori_loop(0, 4, avg_drain, 0)
     for copy in loss_copies:
         copy.wait()
+    for r in range(8):
+        line = jnp.zeros((8, 128), F32)
+        for i in range(4):
+            low = r % 2 * 2 + i // 2
+            line_x, at = (low, r // 2) if i % 2 == 0 else (r // 2, low)
+            row = jnp.broadcast_to(loss_ref[line_x, i % 2 : i % 2 + 1, :], (8, 128))
+            row = pltpu.roll(row, ((i + 4 - at) % 4) * 32, 1)
+            line = jnp.where(lane_group == i, row, line)
+        loss_out[r : r + 1, :] = line[0:1]
 
 
 def per_device(
@@ -508,36 +564,22 @@
     cand_send,
     neg_rows,
 ):
-    core = lax.axis_index("owner") % 2
-    x = lax.axis_index("rep")
-
-    def by_a(lists):
-        lists = lists[0].reshape(4, 4, 2, -1)
-        return jnp.where(core == 1, lists.transpose(1, 0, 2, 3), lists)
-
-    rows = by_a(send_rows).reshape(4, 8, CAP)
-    cands = by_a(cand_send).reshape(4, 1, 256)
-    negs = jnp.broadcast_to(jnp.tile(neg_rows, (1, 4))[None], (4, 1, 128))
-    last = jnp.concatenate([cands, negs, jnp.zeros((4, 1, 128), I32)], axis=2)
-    idx = jnp.concatenate([rows, last, jnp.zeros((4, 7, CAP), I32)], axis=1)
-    grid = cand_author.reshape(4, 4, 2, 32)
-    first = lax.dynamic_index_in_dim(grid[:, :, 0], x, 1, keepdims=False).reshape(1, 128)
-    second = lax.dynamic_index_in_dim(grid[:, :, 1], x, 0, keepdims=False).reshape(1, 128)
-    edges = jnp.concatenate([first, second], axis=1)
-
     vmem = pl.BlockSpec(memory_space=pltpu.VMEM)
+    any_space = pl.BlockSpec(memory_space=pl.ANY)
     dma = pltpu.SemaphoreType.DMA
     out, loss = pl.pallas_call(
         kernel,
         out_shape=(
             jax.ShapeDtypeStruct((W, ROWS), BF),
-            jax.ShapeDtypeStruct((4, 8, 128), F32),
+            jax.ShapeDtypeStruct((8, 128), F32),
         ),
         in_specs=[
             pl.BlockSpec(memory_space=pltpu.SMEM),
+            any_space,
+            any_space,
+            any_space,
+            any_space,
             vmem,
-            vmem,
-            pl.BlockSpec(memory_space=pl.ANY),
             vmem,
             vmem,
             vmem,
@@ -545,6 +587,10 @@
         ],
         out_specs=(vmem, vmem),
         scratch_shapes=[
+            pltpu.VMEM((SLOTS, ROWS), I32),
+            pltpu.VMEM((4, 16, CAP), I32),
+            pltpu.VMEM((32, 128), I32),
+            pltpu.VMEM((4, 8, 128), F32),
             pltpu.VMEM((4, W, ROWS), BF),
             pltpu.VMEM((4, W, ROWS), BF),
             pltpu.VMEM((4, 16, CAP), I32),
@@ -568,6 +614,7 @@
             pltpu.VMEM((D // 2, 256), F32),
             pltpu.VMEM((ROWS, 256), BF),
             dma,
+            dma((3,)),
             dma((4,)),
             dma((4,)),
             dma((4,)),
@@ -602,19 +649,18 @@
         ),
         name="conv_and_score",
     )(
-        tile_src[0],
-        paper_feat,
-        author_feat,
+        tile_src[0].T,
+        paper_feat.T,
+        author_feat.T,
         weights,
+        tile_col[0],
         relation.reshape(6, 128),
-        idx,
-        tile_col[0],
-        edges,
+        send_rows[0],
+        cand_send[0],
+        neg_rows,
+        cand_author.reshape(8, 128),
     )
-    refreshed = out.T
-    even = loss[:, 0].reshape(4, 4, 32).transpose(1, 0, 2)
-    odd = loss[:, 1].reshape(4, 4, 32)
-    return refreshed, jnp.stack([even, odd], axis=2).reshape(-1)
+    return out.T, loss.reshape(-1)
 
 
 def solution(mesh):

time: 117 us -> 106 us (0.906)
  local copies, waits for them, and re-layouts: 11.6 us -> 3.36 us
  other arithmetic: 2.16 us -> 0 us
    unnamed x6 -> x2, local copies, waits for them, and re-layouts: 7.01 us -> 3.36 us
    another operation x5 -> x0, local copies, waits for them, and re-layouts: 1.76 us -> none  [the longest x1 0.88 us: by_a(): lists = lists[0].reshape(4, 4, 2, -1)]
    reshape x6 -> x0, local copies, waits for them, and re-layouts: 1.75 us -> none  [the longest x1 0.77 us: per_device(): grid = cand_author.reshape(4, 4, 2, 32)]
    concatenate x2 -> x0, other arithmetic: 1.3 us -> none  [the longest x1 0.73 us: per_device(): idx = jnp.concatenate([rows, last, jnp.zeros((4, 7, CAP), I32)], axis=1)]
where the time goes in v3:
time: 106 us
  Pallas kernels  102 us (96%)
  local copies, waits for them, and re-layouts  3.36 us (3%)
    pallas_call x1, Pallas kernels, per_device(): pl.pallas_call(kernel, out_shape=(jax.ShapeDtypeStruct((W, ROWS), BF), ja...  102 us
    unnamed x2, local copies, waits for them, and re-layouts  3.36 us

profile of v3, /device:TPU:0, one launch (start us, length us, event | category | flops | bytes accessed | tf_op | source)
XLA Modules:
  0.0 105.5 jit_solution(16679757474075829625)
XLA Ops:
  0.6 101.5 %conv_and_score.1 = (bf16[192,2048]{1,0:T(8,128)(2,1)}, f32[8,128]{1,0:T(8,128)}) custom-call(s32[16,48]{1,0:T(8,128)} %bitcast.18, bf16[192,2048]{1,0:T(8,128)(2,1)} %bitcast.12, bf16[192,2048]{1,0:T(8,128)(2,1)} %bitcast.13, bf16[2,768,768]{2,1,0:T(8,128)(2,1)} %weights_ref.1, s32[48,2048]{1,0:T(8,128)} %bitcast.15, f32[6,128]{1,0:T(8,128)} %bitcast.19, ...), custom_call_target="tpu_custom_call" | custom-call | tf_op jit(solution)/shard_map/conv_and_score/pallas_call | solution.py:570
  102.1 2.1 %copy.14 = bf16[2048,192]{0,1:T(8,128)(2,1)} copy(bf16[2048,192]{0,1:T(8,128)(2,1)} %bitcast.14) | data formatting | bytes 1572864
  104.2 1.3 %copy.15 = f32[1024]{0:T(1024)} copy(f32[1024]{0:T(1024)} %bitcast.21) | data formatting | bytes 8192

commit v4 on v3

--- a/solution.py
+++ b/solution.py
@@ -14,6 +14,13 @@
 ROWS = 2048
 CAP = 512
 HALF = 96
+PARTS = (96, 96)
+STARTS = (0, 96)
+N_PARTS = len(PARTS)
+CHUNKS = 4
+PER = 16 // CHUNKS
+LANES = 128 * PER
+SWAP_AT = 8
 SLOTS = 48
 D = 768
 
@@ -46,57 +53,57 @@
     paper_t,
     author_t,
     idx_all,
-    send_buf,
-    recv_first,
-    recv_second,
-    cand_acc,
-    neg_acc,
-    cand_send,
-    neg_send,
-    cand_rx,
-    cand_all,
-    neg_all,
-    neg_rows,
-    weights_v,
-    weights_t,
-    relation_b,
-    avg_all,
-    self_part,
-    self_sel,
-    avg_sel,
-    edge_hot,
-    w_sem,
-    in_sem,
-    p1_send,
-    p1_recv,
-    f1_send,
-    f1_recv,
-    i1_send,
-    i1_recv,
-    au_send,
-    au_recv,
-    fa_send,
-    fa_recv,
-    main_send,
-    main_recv,
-    cand_ssem,
-    cand_rsem,
-    neg_ssem,
-    neg_rsem,
-    nx_send,
-    nx_recv,
-    swap_send,
-    swap_recv,
-    cx_send,
-    cx_recv,
-    avg_ssem,
-    avg_rsem,
-    fw_ssem,
-    fw_rsem,
-    loss_ssem,
-    loss_rsem,
+    *rest,
 ):
-    recv = (recv_first, recv_second)
+    (send_buf, recv, weights_t, avg_all, avg_sel), rest = (
+        [rest[i * N_PARTS : (i + 1) * N_PARTS] for i in range(5)],
+        rest[5 * N_PARTS :],
+    )
+    (
+        cand_acc,
+        neg_acc,
+        cand_send,
+        neg_send,
+        cand_rx,
+        cand_all,
+        neg_all,
+        neg_rows,
+        weights_v,
+        relation_b,
+        self_part,
+        self_sel,
+        edge_hot,
+        w_sem,
+        in_sem,
+        p1_send,
+        p1_recv,
+        f1_send,
+        f1_recv,
+        i1_send,
+        i1_recv,
+        au_send,
+        au_recv,
+        fa_send,
+        fa_recv,
+        main_send,
+        main_recv,
+        cand_ssem,
+        cand_rsem,
+        neg_ssem,
+        neg_rsem,
+        nx_send,
+        nx_recv,
+        swap_send,
+        swap_recv,
+        cx_send,
+        cx_recv,
+        avg_ssem,
+        avg_rsem,
+        fw_ssem,
+        fw_rsem,
+        loss_ssem,
+        loss_rsem,
+    ) = rest
     owner = lax.axis_index("owner")
     x = lax.axis_index("rep")
     core = owner % 2
@@ -210,12 +217,16 @@
     for dx in (1, 3):
         author_copy(dx).start()
 
+    def place_of(k):
+        own = k // 6
+        j = k % 3
+        return (1 - own) * (1 + 2 * j - 3 * (j // 2)), (1 - own) * (k // 3) + own * (k - 6)
+
     def main_copy(da, k, h):
-        db = (k // 2 + 1) % 4
-        dcore = k % 2
+        db, dcore = place_of(k)
         source = owner_at((a + da) % 4, b, core)
         return remote(
-            send_buf.at[da, k, h],
+            send_buf[h].at[da, k],
             recv[h].at[pl.ds(4 * source, 4)],
             main_send.at[h, da, k],
             main_recv.at[h, source],
@@ -227,7 +238,7 @@
         def _():
             source = owner_at((a + da) % 4, b, core)
             pltpu.make_async_copy(
-                send_buf.at[da, k, h], recv[h].at[pl.ds(4 * source, 4)], main_recv.at[h, source]
+                send_buf[h].at[da, k], recv[h].at[pl.ds(4 * source, 4)], main_recv.at[h, source]
             ).start()
 
         @pl.when(k != 6)
@@ -236,12 +247,14 @@
 
     def select_main(da):
         def step(k, carry):
-            row = ((b + k // 2 + 1) % 4) * 2 + (core + k) % 2
+            db, dcore = place_of(k)
+            row = ((b + db) % 4) * 2 + (core + dcore) % 2
             picks = idx_all[da, pl.ds(row, 1), :]
             out = jnp.dot(paper_t[da], one_hot(ROWS, picks), preferred_element_type=F32).astype(BF)
-            for h in range(2):
+            for h in range(N_PARTS):
                 for j in range(4):
-                    send_buf[da, k, h, j] = out[h * HALF : (h + 1) * HALF, j * 128 : (j + 1) * 128]
+                    rows = out[STARTS[h] : STARTS[h] + PARTS[h], j * 128 : (j + 1) * 128]
+                    send_buf[h][da, k, j] = rows
             main_start(da, k, 0)
             return carry
 
@@ -263,12 +276,13 @@
         neg_acc[...] = jnp.where(here, out[:, 256:384], old)
 
     def cand_copy(k):
+        db, dcore = place_of(k)
         return remote(
-            cand_send.at[((b + k // 2 + 1) % 4) * 2 + (core + k) % 2],
+            cand_send.at[((b + db) % 4) * 2 + (core + dcore) % 2],
             cand_rx.at[b, core],
             cand_ssem.at[k],
             cand_rsem.at[b * 2 + core],
-            device(db=(k // 2 + 1) % 4, dcore=k % 2),
+            device(db=db, dcore=dcore),
         )
 
     def cand_local():
@@ -288,9 +302,9 @@
     select_extra(0)
     weights_copy.wait()
     for w in range(2):
-        for h in range(2):
-            rows = [weights_v[w, pl.ds(i * W + h * HALF, HALF), :] for i in range(4)]
-            weights_t[w, h] = jnp.transpose(jnp.concatenate(rows, axis=0))
+        for h in range(N_PARTS):
+            rows = [weights_v[w, pl.ds(i * W + STARTS[h], PARTS[h]), :] for i in range(4)]
+            weights_t[h][w] = jnp.transpose(jnp.concatenate(rows, axis=0))
     for i in range(6):
         row = jnp.broadcast_to(relation_ref[i : i + 1, :], (128, 128))
         relation_b[pl.ds(i * 128, 128), :] = jnp.transpose(row)
@@ -312,11 +326,7 @@
     select_main(1)
     select_extra(1)
     row_list(1).wait_recv()
-    select_main(3)
     select_extra(3)
-    for dx in (1, 3):
-        author_copy(dx).wait_recv()
-        author_forward(dx).start()
     row_list(2).wait_recv()
     for da in (1, 3):
         paper_forward(da).wait_recv()
@@ -330,14 +340,10 @@
     for k in (0, 1, 2, 3, 4, 5, 7):
         cand_copy(k).start()
     cand_local().start()
-    select_main(2)
-
-    def second_half(k, carry):
-        for da in (0, 1, 3, 2):
-            main_start(da, k, 1)
-        return carry
-
-    lax.fori_loop(0, 8, second_half, 0)
+    for dx in (1, 3):
+        author_copy(dx).wait_recv()
+        author_forward(dx).start()
+    select_main(3)
 
     for slot in range(4):
         pltpu.make_async_copy(neg_send, neg_all.at[core, x, slot], neg_rsem.at[slot]).wait()
@@ -360,13 +366,26 @@
     for copy in cand_x:
         copy.start()
     cand_all[x] = cand_rx[x]
+    select_main(2)
+
+    def later_part(h):
+        def step(k, carry):
+            for da in (0, 1, 3, 2):
+                main_start(da, k, h)
+            return carry
+
+        lax.fori_loop(0, 8, step, 0)
+
+    for h in range(1, N_PARTS):
+        later_part(h)
 
     def avg_copy(h, g, dx):
-        part = avg_all.at[h, x, g]
+        part = avg_all[h].at[x, g]
         return remote(part, part, avg_ssem.at[h, g, dx], avg_rsem.at[h, g, dx], device(dx=dx))
 
     def avg_forward(h, g, dx):
-        part = avg_all.at[h, (x + 4 - dx) % 4, g, pl.ds(0 if dx == 1 else HALF // 2, HALF // 2)]
+        size = PARTS[h] // 2
+        part = avg_all[h].at[(x + 4 - dx) % 4, g, pl.ds(0 if dx == 1 else size, size)]
         return remote(part, part, fw_ssem.at[h, g, dx], fw_rsem.at[h, g, dx], device(dx=dx))
 
     def pass_on(h, g):
@@ -374,10 +393,10 @@
             avg_copy(h, g, dx).wait_recv()
             avg_forward(h, g, dx).start()
 
-    def aggregate(h):
+    def aggregate(h, between):
         def recv_wait(s, carry):
             pltpu.make_async_copy(
-                send_buf.at[0, 0, h], recv[h].at[pl.ds(4 * s, 4)], main_recv.at[h, s]
+                send_buf[h].at[0, 0], recv[h].at[pl.ds(4 * s, 4)], main_recv.at[h, s]
             ).wait()
             return carry
 
@@ -387,7 +406,7 @@
             lanes = pl.ds(pl.multiple_of(block * 128, 128), 128)
             live = (col_ref[:, lanes] < 128).astype(F32)
             scale = 1.0 / jnp.maximum(jnp.sum(live, axis=0, keepdims=True), 1.0)
-            total = jnp.zeros((HALF, 128), F32)
+            total = jnp.zeros((PARTS[h], 128), F32)
             for t in range(0, SLOTS, 8):
                 left = [recv[h][src_ref[block, t + i]] for i in range(8)]
                 right = [one_hot(128, col_ref[t + i : t + i + 1, lanes]) for i in range(8)]
@@ -396,91 +415,102 @@
                     jnp.concatenate(right, axis=0),
                     preferred_element_type=F32,
                 )
-            g = block // 4
-            inner = pl.ds(pl.multiple_of((block % 4) * 128, 128), 128)
-            avg_all[h, x, g, :, inner] = (total * scale).astype(BF)
-
-            @pl.when(block % 4 == 3)
+            g = block // PER
+            inner = pl.ds(pl.multiple_of((block % PER) * 128, 128), 128)
+            avg_all[h][x, g, :, inner] = (total * scale).astype(BF)
+
+            @pl.when(block % PER == PER - 1)
             def _():
                 for dx in (1, 3):
                     avg_copy(h, g, dx).start()
 
-            @pl.when(block % 4 == 3)
+            @pl.when(block % PER == PER - 1)
             def _():
                 @pl.when(g >= 2)
                 def _():
                     pass_on(h, g - 2)
 
+            for at, call in between:
+                pl.when(block == at)(call)
             return carry
 
         lax.fori_loop(0, 16, step, 0)
 
-    aggregate(0)
+    aggregate(0, [])
 
     own_rows = pl.ds(pl.multiple_of(x * W, 16), W)
-    pass_on(0, 2)
+    pass_on(0, CHUNKS - 2)
     for dx in (1, 3):
         author_forward(dx).wait_recv()
     for g in range(4):
         lanes = pl.ds(g * 512, 512)
         total = jnp.zeros((W, 512), F32)
-        for h in range(2):
-            block = [author_t[i, pl.ds(h * HALF, HALF), lanes] for i in range(4)]
+        for h in range(N_PARTS):
+            block = [author_t[i, pl.ds(STARTS[h], PARTS[h]), lanes] for i in range(4)]
             total = total + jnp.dot(
-                weights_t[0, h, own_rows, :],
+                weights_t[h][0, own_rows, :],
                 jnp.concatenate(block, axis=0),
                 preferred_element_type=F32,
             )
         self_part[:, lanes] = total
-    pass_on(0, 3)
+    pass_on(0, CHUNKS - 1)
     author_sel = [
         jnp.dot(author_t[i], edge_hot[...], preferred_element_type=F32).astype(BF) for i in range(4)
     ]
     total = jnp.zeros((D, 256), F32)
-    for h in range(2):
-        block = [author_sel[i][h * HALF : (h + 1) * HALF] for i in range(4)]
+    for h in range(N_PARTS):
+        block = [author_sel[i][STARTS[h] : STARTS[h] + PARTS[h]] for i in range(4)]
         total = total + jnp.dot(
-            weights_t[0, h], jnp.concatenate(block, axis=0), preferred_element_type=F32
+            weights_t[h][0], jnp.concatenate(block, axis=0), preferred_element_type=F32
         )
     self_sel[...] = total
-    for copy in neg_x:
-        copy.wait_recv()
     swap = remote(neg_all.at[core], neg_all.at[core], swap_send, swap_recv, device(dcore=1))
-    swap.start()
+
+    def swap_cores():
+        for copy in neg_x:
+            copy.wait_recv()
+        swap.start()
+
+    def dense(h):
+        avg_sel[h][...] = jnp.zeros_like(avg_sel[h])
+
+        def step(g, carry):
+            for dx in (1, 3):
+                avg_forward(h, g, dx).wait_recv()
+            lanes = pl.ds(pl.multiple_of(g * LANES, LANES), LANES)
+            block = jnp.concatenate([avg_all[h][i, g] for i in range(4)], axis=0)
+            mixed = self_part[:, lanes] + jnp.dot(
+                weights_t[h][1, own_rows, :], block, preferred_element_type=F32
+            )
+            if h < N_PARTS - 1:
+                self_part[:, lanes] = mixed
+            else:
+                out_ref[:, lanes] = mixed.astype(BF)
+            hot = edge_hot[lanes, :]
+            avg_sel[h][...] += jnp.dot(block, hot, preferred_element_type=F32)
+            return carry
+
+        lax.fori_loop(0, CHUNKS, step, 0)
+        return jnp.dot(weights_t[h][1], avg_sel[h][...].astype(BF), preferred_element_type=F32)
+
+    for h in range(1, N_PARTS):
+        between = []
+        if h > 1:
+            between.append((3, lambda: pass_on(h - 1, CHUNKS - 2)))
+            between.append((7, lambda: pass_on(h - 1, CHUNKS - 1)))
+        if h == 1:
+            between.append((SWAP_AT, swap_cores))
+        aggregate(h, between)
+    pass_on(N_PARTS - 1, CHUNKS - 2)
     swap.wait()
     for c in range(2):
         for i in range(4):
             block = jnp.concatenate([neg_all[c, j, i] for j in range(4)], axis=0)
             neg_rows[pl.ds((c * 4 + i) * 128, 128), :] = jnp.transpose(block)
-
-    aggregate(1)
-    pass_on(1, 2)
-
-    def dense(h):
-        avg_sel[...] = jnp.zeros_like(avg_sel)
-
-        def step(g, carry):
-            for dx in (1, 3):
-                avg_forward(h, g, dx).wait_recv()
-            lanes = pl.ds(pl.multiple_of(g * 512, 512), 512)
-            block = jnp.concatenate([avg_all[h, i, g] for i in range(4)], axis=0)
-            mixed = self_part[:, lanes] + jnp.dot(
-                weights_t[1, h, own_rows, :], block, preferred_element_type=F32
-            )
-            if h == 0:
-                self_part[:, lanes] = mixed
-            else:
-                out_ref[:, lanes] = mixed.astype(BF)
-            hot = edge_hot[pl.ds(pl.multiple_of(g * 512, 512), 512), :]
-            avg_sel[...] += jnp.dot(block, hot, preferred_element_type=F32)
-            return carry
-
-        lax.fori_loop(0, 4, step, 0)
-        return jnp.dot(weights_t[1, h], avg_sel[...].astype(BF), preferred_element_type=F32)
-
-    self_sel[...] += dense(0)
-    pass_on(1, 3)
-    refreshed = self_sel[...] + dense(1)
+    pass_on(N_PARTS - 1, CHUNKS - 1)
+    for h in range(N_PARTS - 1):
+        self_sel[...] += dense(h)
+    refreshed = self_sel[...] + dense(N_PARTS - 1)
 
     gain = jnp.concatenate([relation_b[...]] * 2, axis=1)
     queries = (refreshed.astype(BF).astype(F32) * gain).astype(BF)
@@ -523,7 +553,7 @@
     def main_drain(k, carry):
         @pl.when(k != 6)
         def _():
-            for h in range(2):
+            for h in range(N_PARTS):
                 for da in range(4):
                     main_copy(da, k, h).wait_send()
 
@@ -532,13 +562,13 @@
     lax.fori_loop(0, 8, main_drain, 0)
 
     def avg_drain(g, carry):
-        for h in range(2):
+        for h in range(N_PARTS):
             for dx in (1, 3):
                 avg_copy(h, g, dx).wait_send()
                 avg_forward(h, g, dx).wait_send()
         return carry
 
-    lax.fori_loop(0, 4, avg_drain, 0)
+    lax.fori_loop(0, CHUNKS, avg_drain, 0)
     for copy in loss_copies:
         copy.wait()
     for r in range(8):
@@ -594,9 +624,11 @@
             pltpu.VMEM((4, W, ROWS), BF),
             pltpu.VMEM((4, W, ROWS), BF),
             pltpu.VMEM((4, 16, CAP), I32),
-            pltpu.VMEM((4, 8, 2, 4, HALF, 128), BF),
-            pltpu.VMEM((128, HALF, 128), BF),
-            pltpu.VMEM((128, HALF, 128), BF),
+            *[pltpu.VMEM((4, 8, 4, n, 128), BF) for n in PARTS],
+            *[pltpu.VMEM((128, n, 128), BF) for n in PARTS],
+            *[pltpu.VMEM((2, D, 4 * n), BF) for n in PARTS],
+            *[pltpu.VMEM((4, CHUNKS, n, LANES), BF) for n in PARTS],
+            *[pltpu.VMEM((4 * n, 256), F32) for n in PARTS],
             pltpu.VMEM((8, W, 128), F32),
             pltpu.VMEM((W, 128), F32),
             pltpu.VMEM((8, W, 128), BF),
@@ -606,12 +638,9 @@
             pltpu.VMEM((2, 4, 4, W, 128), BF),
             pltpu.VMEM((1024, D), BF),
             pltpu.VMEM((2, D, D), BF),
-            pltpu.VMEM((2, 2, D, D // 2), BF),
             pltpu.VMEM((D, 128), F32),
-            pltpu.VMEM((2, 4, 4, HALF, 512), BF),
             pltpu.VMEM((W, ROWS), F32),
             pltpu.VMEM((D, 256), F32),
-            pltpu.VMEM((D // 2, 256), F32),
             pltpu.VMEM((ROWS, 256), BF),
             dma,
             dma((3,)),
@@ -625,8 +654,8 @@
             dma((4,)),
             dma((4,)),
             dma((4,)),
-            dma((2, 4, 8)),
-            dma((2, 32)),
+            dma((N_PARTS, 4, 8)),
+            dma((N_PARTS, 32)),
             dma((8,)),
             dma((8,)),
             dma((4,)),
@@ -637,10 +666,10 @@
             dma,
             dma((4,)),
             dma((4,)),
-            dma((2, 4, 4)),
-            dma((2, 4, 4)),
-            dma((2, 4, 4)),
-            dma((2, 4, 4)),
+            dma((N_PARTS, CHUNKS, 4)),
+            dma((N_PARTS, CHUNKS, 4)),
+            dma((N_PARTS, CHUNKS, 4)),
+            dma((N_PARTS, CHUNKS, 4)),
             dma((4,)),
             dma((4,)),
         ],

time: 106 us -> 101 us (0.953)
  Pallas kernels: 102 us -> 96.9 us
    pallas_call x1, Pallas kernels: 102 us -> 96.9 us  [per_device(): pl.pallas_call(kernel, out_shape=(jax.ShapeDtypeStruct((W, ROWS), BF), ja...]
where the time goes in v4:
time: 101 us
  Pallas kernels  96.9 us (96%)
  local copies, waits for them, and re-layouts  3.36 us (3%)
    pallas_call x1, Pallas kernels, per_device(): pl.pallas_call(kernel, out_shape=(jax.ShapeDtypeStruct((W, ROWS), BF), ja...  96.9 us
    unnamed x2, local copies, waits for them, and re-layouts  3.36 us

profile of v4, /device:TPU:0, one launch (start us, length us, event | category | flops | bytes accessed | tf_op | source)
XLA Modules:
  0.0 100.9 jit_solution(10614144415371943594)
XLA Ops:
  0.6 96.9 %conv_and_score.1 = (bf16[192,2048]{1,0:T(8,128)(2,1)}, f32[8,128]{1,0:T(8,128)}) custom-call(s32[16,48]{1,0:T(8,128)} %bitcast.18, bf16[192,2048]{1,0:T(8,128)(2,1)} %bitcast.12, bf16[192,2048]{1,0:T(8,128)(2,1)} %bitcast.13, bf16[2,768,768]{2,1,0:T(8,128)(2,1)} %weights_ref.1, s32[48,2048]{1,0:T(8,128)} %bitcast.15, f32[6,128]{1,0:T(8,128)} %bitcast.19, ...), custom_call_target="tpu_custom_call" | custom-call | tf_op jit(solution)/shard_map/conv_and_score/pallas_call | solution.py:600
  97.6 2.1 %copy.14 = bf16[2048,192]{0,1:T(8,128)(2,1)} copy(bf16[2048,192]{0,1:T(8,128)(2,1)} %bitcast.14) | data formatting | bytes 1572864
  99.6 1.3 %copy.15 = f32[1024]{0:T(1024)} copy(f32[1024]{0:T(1024)} %bitcast.21) | data formatting | bytes 8192

commit v5 on v4

--- a/solution.py
+++ b/solution.py
@@ -426,9 +426,9 @@
 
             @pl.when(block % PER == PER - 1)
             def _():
-                @pl.when(g >= 2)
+                @pl.when(g >= 3)
                 def _():
-                    pass_on(h, g - 2)
+                    pass_on(h, g - 3)
 
             for at, call in between:
                 pl.when(block == at)(call)
@@ -439,6 +439,7 @@
     aggregate(0, [])
 
     own_rows = pl.ds(pl.multiple_of(x * W, 16), W)
+    pass_on(0, CHUNKS - 3)
     pass_on(0, CHUNKS - 2)
     for dx in (1, 3):
         author_forward(dx).wait_recv()
@@ -501,6 +502,7 @@
         if h == 1:
             between.append((SWAP_AT, swap_cores))
         aggregate(h, between)
+    pass_on(N_PARTS - 1, CHUNKS - 3)
     pass_on(N_PARTS - 1, CHUNKS - 2)
     swap.wait()
     for c in range(2):
@@ -689,6 +691,20 @@
         neg_rows,
         cand_author.reshape(8, 128),
     )
+    def hand_over(out_in, loss_in, out_to, loss_to):
+        out_to[...] = out_in[...]
+        loss_to[...] = loss_in[...]
+
+    out, loss = pl.pallas_call(
+        hand_over,
+        out_shape=(
+            jax.ShapeDtypeStruct((W, ROWS), BF),
+            jax.ShapeDtypeStruct((8, 128), F32),
+        ),
+        in_specs=[vmem, vmem],
+        out_specs=(vmem, vmem),
+        name="hand_over",
+    )(out, loss)
     return out.T, loss.reshape(-1)
 
 

time: 101 us -> 98.2 us (0.972)
  local copies, waits for them, and re-layouts: 3.36 us -> 0 us
    unnamed x2 -> x0, local copies, waits for them, and re-layouts: 3.36 us -> none
    pallas_call x0 -> x1, Pallas kernels: none -> 2.07 us  [per_device(): pl.pallas_call(hand_over, out_shape=(jax.ShapeDtypeStruct((W, ROWS), BF),...]
    pallas_call x1, Pallas kernels: 96.9 us -> 95.3 us  [per_device(): pl.pallas_call(kernel, out_shape=(jax.ShapeDtypeStruct((W, ROWS), BF), ja...]
where the time goes in v5:
time: 98.2 us; the launch traced here: 98 us
  Pallas kernels  97.4 us (99%)
    pallas_call x1, Pallas kernels, per_device(): pl.pallas_call(kernel, out_shape=(jax.ShapeDtypeStruct((W, ROWS), BF), ja...  95.3 us
    pallas_call x1, Pallas kernels, per_device(): pl.pallas_call(hand_over, out_shape=(jax.ShapeDtypeStruct((W, ROWS), BF),...  2.07 us

profile of v5, /device:TPU:0, one launch (start us, length us, event | category | flops | bytes accessed | tf_op | source)
XLA Modules:
  0.0 98.0 jit_solution(5820693736185138461)
XLA Ops:
  0.6 95.3 %conv_and_score.1 = (bf16[192,2048]{1,0:T(8,128)(2,1)}, f32[8,128]{1,0:T(8,128)}) custom-call(s32[16,48]{1,0:T(8,128)} %bitcast.17, bf16[192,2048]{1,0:T(8,128)(2,1)} %bitcast.12, bf16[192,2048]{1,0:T(8,128)(2,1)} %bitcast.13, bf16[2,768,768]{2,1,0:T(8,128)(2,1)} %weights_ref.1, s32[48,2048]{1,0:T(8,128)} %bitcast.14, f32[6,128]{1,0:T(8,128)} %bitcast.18, ...), custom_call_target="tpu_custom_call" | custom-call | tf_op jit(solution)/shard_map/conv_and_score/pallas_call | solution.py:602
  96.0 2.1 %hand_over.1 = (bf16[192,2048]{1,0:T(8,128)(2,1)}, f32[8,128]{1,0:T(8,128)}) custom-call(bf16[192,2048]{1,0:T(8,128)(2,1)} %get-tuple-element.6.out_in, f32[8,128]{1,0:T(8,128)} %get-tuple-element.7.loss_in), custom_call_target="tpu_custom_call" | custom-call | tf_op jit(solution)/shard_map/hand_over/pallas_call | solution.py:698

commit v6 on v5

--- a/solution.py
+++ b/solution.py
@@ -324,6 +324,9 @@
         paper_forward(da).start()
     row_list(3).wait_recv()
     select_main(1)
+    for dx in (1, 3):
+        author_copy(dx).wait_recv()
+        author_forward(dx).start()
     select_extra(1)
     row_list(1).wait_recv()
     select_extra(3)
@@ -340,9 +343,6 @@
     for k in (0, 1, 2, 3, 4, 5, 7):
         cand_copy(k).start()
     cand_local().start()
-    for dx in (1, 3):
-        author_copy(dx).wait_recv()
-        author_forward(dx).start()
     select_main(3)
 
     for slot in range(4):

time: 98.2 us -> 98.1 us (level)
  no operation moved by 1% of the time
where the time goes in v6:
time: 98.1 us; the launch traced here: 97.9 us
  Pallas kernels  97.3 us (99%)
    pallas_call x1, Pallas kernels, per_device(): pl.pallas_call(kernel, out_shape=(jax.ShapeDtypeStruct((W, ROWS), BF), ja...  95.2 us
    pallas_call x1, Pallas kernels, per_device(): pl.pallas_call(hand_over, out_shape=(jax.ShapeDtypeStruct((W, ROWS), BF),...  2.07 us

profile of v6, /device:TPU:0, one launch (start us, length us, event | category | flops | bytes accessed | tf_op | source)
XLA Modules:
  0.0 97.9 jit_solution(6076089175585937978)
XLA Ops:
  0.6 95.2 %conv_and_score.1 = (bf16[192,2048]{1,0:T(8,128)(2,1)}, f32[8,128]{1,0:T(8,128)}) custom-call(s32[16,48]{1,0:T(8,128)} %bitcast.17, bf16[192,2048]{1,0:T(8,128)(2,1)} %bitcast.12, bf16[192,2048]{1,0:T(8,128)(2,1)} %bitcast.13, bf16[2,768,768]{2,1,0:T(8,128)(2,1)} %weights_ref.1, s32[48,2048]{1,0:T(8,128)} %bitcast.14, f32[6,128]{1,0:T(8,128)} %bitcast.18, ...), custom_call_target="tpu_custom_call" | custom-call | tf_op jit(solution)/shard_map/conv_and_score/pallas_call | solution.py:602
  95.9 2.1 %hand_over.1 = (bf16[192,2048]{1,0:T(8,128)(2,1)}, f32[8,128]{1,0:T(8,128)}) custom-call(bf16[192,2048]{1,0:T(8,128)(2,1)} %get-tuple-element.6.out_in, f32[8,128]{1,0:T(8,128)} %get-tuple-element.7.loss_in), custom_call_target="tpu_custom_call" | custom-call | tf_op jit(solution)/shard_map/hand_over/pallas_call | solution.py:698
